TPU v7x, 32 devices: a whole 2x2x4 slice. The times are simulated.
32 devices in a mesh: dp: 8 (over y, x, core), shard: 4 (over z).
Axes of the slice: x: 2, y: 2, z: 4, core: 2. Of those that a mesh axis runs over, the one named last changes fastest.
Arguments:
- tokens: bfloat16 [32768, 768], P(('dp', 'shard'))
- out_grad: bfloat16 [32768, 768], P(('dp', 'shard'))
- first_lengths: int32 [32], P(('dp', 'shard')), may hold values from 512 to 1024, as said below
- quant_scales: float32 [6], replicated, as said below
- attn_quant: bfloat16 [768, 3072], P('dp', 'shard'), may hold values from -127 to 127
- up_quant: bfloat16 [768, 3072], P('dp', 'shard'), may hold values from -127 to 127
- down_quant: bfloat16 [3072, 768], P('dp', 'shard'), may hold values from -127 to 127
- attn_master: float32 [768, 3072], P('dp', 'shard'), as said below
- attn_first: float32 [768, 3072], P('dp', 'shard')
- attn_second: float32 [768, 3072], P('dp', 'shard'), as said below
- attn_average: float32 [768, 3072], P('dp', 'shard'), may hold values from -0.21875 to 0.21875
- up_master: float32 [768, 3072], P('dp', 'shard'), as said below
- up_first: float32 [768, 3072], P('dp', 'shard')
- up_second: float32 [768, 3072], P('dp', 'shard'), as said below
- up_average: float32 [768, 3072], P('dp', 'shard'), may hold values from -0.21875 to 0.21875
- down_master: float32 [3072, 768], P('dp', 'shard'), as said below
- down_first: float32 [3072, 768], P('dp', 'shard')
- down_second: float32 [3072, 768], P('dp', 'shard'), as said below
- down_average: float32 [3072, 768], P('dp', 'shard'), may hold values from -0.109375 to 0.109375
- vector_master: float32 [768, 12], P('dp', 'shard')
- vector_first: float32 [768, 12], P('dp', 'shard')
- vector_second: float32 [768, 12], P('dp', 'shard'), as said below
- vector_average: float32 [768, 12], P('dp', 'shard'), may hold values from -3 to 3
Outputs:
- layer_out: bfloat16 [32768, 768], P(('dp', 'shard'))
- input_grad: bfloat16 [32768, 768], P(('dp', 'shard'))
- grad_norm: float32 [], replicated
- attn_first_new: float32 [768, 3072], P('dp', 'shard')
- attn_second_new: float32 [768, 3072], P('dp', 'shard')
- attn_master_new: float32 [768, 3072], P('dp', 'shard')
- attn_average_new: float32 [768, 3072], P('dp', 'shard')
- up_first_new: float32 [768, 3072], P('dp', 'shard')
- up_second_new: float32 [768, 3072], P('dp', 'shard')
- up_master_new: float32 [768, 3072], P('dp', 'shard')
- up_average_new: float32 [768, 3072], P('dp', 'shard')
- down_first_new: float32 [3072, 768], P('dp', 'shard')
- down_second_new: float32 [3072, 768], P('dp', 'shard')
- down_master_new: float32 [3072, 768], P('dp', 'shard')
- down_average_new: float32 [3072, 768], P('dp', 'shard')
- vector_first_new: float32 [768, 12], P('dp', 'shard')
- vector_second_new: float32 [768, 12], P('dp', 'shard')
- vector_master_new: float32 [768, 12], P('dp', 'shard')
- vector_average_new: float32 [768, 12], P('dp', 'shard')
Inputs may be any that keep to these rules, and one draw needn't show every extreme that they name: `first_lengths`: each buffer of 1024 rows holds one sequence of 1024 tokens (value 1024) or two of 512 tokens (value 1024 / 2); both kinds occur in every draw. `quant_scales`: positive. `attn_master`: each entry within half a quantization step of the integer copy times its scale. `up_master`: each entry within half a quantization step of the integer copy times its scale. `down_master`: each entry within half a quantization step of the integer copy times its scale. `attn_second`: positive. `up_second`: positive. `down_second`: positive. `vector_second`: positive.
All inputs are finite; a program needn't handle non-finite values.
Results may differ from a plain program's by a relative error of at most 0.012.
Values may be sent and summed in bfloat16 or wider, within the bound.
No kernel may reach another device: no remote copies, remote signals or barrier semaphores. Data moves between devices by JAX's collectives and lax.ppermute only.
A program may use at most 256 MiB of HBM per device.

v0:
```python
import functools
import math

import jax
import jax.numpy as jnp
from jax import lax
from jax.experimental import pallas as pl
from jax.experimental.pallas import tpu as pltpu
from jax.sharding import PartitionSpec as P

HEAD_DIM = 64
STEP = 10

norm_eps = 1e-06
clip_limit = 1.0
beta_first = 0.9
beta_second = 0.999
adam_eps = 1e-08
matrix_rate = 0.08
vector_rate = 0.5
matrix_decay = 0.01
average_keep = 0.9

VMEM = 62 * 2**20
GELU_K = math.sqrt(2.0 / math.pi)
GELU_C = 0.044715
f32 = jnp.float32
bf16 = jnp.bfloat16
SDS = jax.ShapeDtypeStruct


def dot(left, right):
    return jnp.dot(left, right, preferred_element_type=f32)


def dot_last(left, right):
    return lax.dot_general(left, right, (((1,), (1,)), ((), ())), preferred_element_type=f32)


def col_sum(value):
    return jnp.sum(value, axis=0, keepdims=True)


def params(**extra):
    return pltpu.CompilerParams(vmem_limit_bytes=VMEM, **extra)


def cost(flops, moved, trans=0):
    return pl.CostEstimate(flops=int(flops), bytes_accessed=int(moved), transcendentals=int(trans))


SMEM = pl.BlockSpec(memory_space=pltpu.SMEM)
ANY = pl.BlockSpec(memory_space=pl.ANY)


def piece_row(place_ref, index, count):
    if count == 1:
        return 0
    half = count // 2
    return ((place_ref[1] ^ (index % half)) * 2) + (place_ref[0] ^ (index // half))


def block_copies(place_ref, pieces, blocks, dest, sems):
    count = len(pieces)
    rows, width = dest.shape[0] // count, pieces[0].shape[1]

    def copy(at, block, index):
        def make():
            row = pl.multiple_of(piece_row(place_ref, index, count) * rows, 16)
            return pltpu.make_async_copy(
                pieces[index].at[block * rows : (block + 1) * rows],
                dest.at[pl.ds(row, rows), at * width : (at + 1) * width],
                sems.at[at * count + index],
            )

        return make

    return [copy(at, block, index) for at, block in enumerate(blocks) for index in range(count)]


def some_copies(copies, part, parts):
    size = len(copies) // parts
    return copies[part * size : (part + 1) * size]


def down_copies(place_ref, sources, dest, sems):
    slots, spots, rows, width = sources[0].shape
    count = len(sources)

    def copy(spot, core, slot):
        def make():
            col = (spot * count + (place_ref[0] ^ core)) * width
            return pltpu.make_async_copy(
                sources[core].at[slot, spot],
                dest.at[slot * rows : (slot + 1) * rows, pl.ds(pl.multiple_of(col, 128), width)],
                sems.at[(spot * count + core) * slots + slot],
            )

        return make

    return [copy(spot, core, slot) for spot in range(spots) for core in range(count) for slot in range(slots)]


def start_all(copies):
    for copy in copies:
        copy().start()


def wait_all(copies):
    for copy in copies:
        copy().wait()


def normalize(value):
    centre = value - jnp.mean(value, axis=-1, keepdims=True)
    inv_std = lax.rsqrt(jnp.mean(centre * centre, axis=-1, keepdims=True) + norm_eps)
    return centre * inv_std, inv_std


def normalize_back(scaled, normed, inv_std):
    return inv_std * (
        scaled
        - jnp.mean(scaled, axis=-1, keepdims=True)
        - normed * jnp.mean(scaled * normed, axis=-1, keepdims=True)
    )


def attn_stack_kernel(place_ref, *refs):
    blocks, qkv_ref, out_ref = refs[:4], refs[-2], refs[-1]
    rows = out_ref.shape[0]
    vectors = None
    for slot, block in enumerate(blocks):
        plane = slot ^ place_ref[2]
        more = pltpu.roll(block[rows:, :].astype(f32), 3 * plane, 0)
        vectors = more if vectors is None else vectors + more

        @pl.when(plane < 3)
        def _():
            qkv_ref[pl.ds(pl.multiple_of(plane * rows, 16), rows), :] = block[:rows, :]

        @pl.when(plane == 3)
        def _():
            out_ref[...] = block[:rows, :]

    qkv_ref[3 * rows :, :] = vectors.astype(bf16)


def attn_stack(place, blocks, deps):
    rows, width = blocks[0].shape
    rows -= 16
    return pl.pallas_call(
        attn_stack_kernel,
        in_specs=[SMEM] + [pl.BlockSpec(memory_space=pltpu.VMEM)] * 4 + [ANY] * len(deps),
        out_specs=[pl.BlockSpec(memory_space=pltpu.VMEM)] * 2,
        out_shape=[SDS((3 * rows + 16, width), bf16), SDS((rows, width), bf16)],
        compiler_params=params(),
        cost_estimate=cost(1e6, 1e6),
        name="attention_weight_order",
    )(place, *blocks, *deps)


def stack_kernel(place_ref, *refs, which, extra):
    blocks, out_ref = refs[:4], refs[-1]
    rows = blocks[0].shape[0]
    for slot, block in enumerate(blocks):
        at = pl.multiple_of((slot ^ place_ref[which]) * rows, 16)
        out_ref[pl.ds(at, rows), :] = block[...]
    if extra:
        out_ref[4 * rows :, :] = refs[4][...]


def stack(place, blocks, which, *extra, deps=()):
    rows, width = blocks[0].shape
    return pl.pallas_call(
        functools.partial(stack_kernel, which=which, extra=len(extra)),
        in_specs=[SMEM] + [pl.BlockSpec(memory_space=pltpu.VMEM)] * (4 + len(extra)) + [ANY] * len(deps),
        out_specs=pl.BlockSpec(memory_space=pltpu.VMEM),
        out_shape=SDS((rows * (4 + len(extra)), width), bf16),
        compiler_params=params(),
        cost_estimate=cost(1e6, 1e6),
        name="weight_order",
    )(place, *blocks, *extra, *deps)


def attn_fwd_kernel(place_ref, len_ref, scale_ref, *refs, block, count, deps):
    pieces = refs[:count]
    refs = refs[:count] + refs[count + deps :]
    x_ref, q_ref, k_ref, v_ref, c_ref, lse_ref, vec_ref, w_ref, packed, sems, vec_sems = refs[count:]
    rows, width = q_ref.shape
    total_width = x_ref.shape[1]
    group = pl.program_id(0)
    weights = block_copies(place_ref, pieces, range(3), w_ref, sems)

    @pl.when(group == 0)
    def _():
        top = pieces[0].shape[0] - 16
        vec_copies = [
            pltpu.make_async_copy(piece.at[top : top + 16], packed.at[index], vec_sems.at[index])
            for index, piece in enumerate(pieces)
        ]
        for copy in vec_copies:
            copy.start()
        start_all(weights)
        for copy in vec_copies:
            copy.wait()
        vectors = None
        for index in range(count):
            shift = piece_row(place_ref, index, count) * (total_width // count)
            more = packed[index].astype(f32)
            more = more if count == 1 else pltpu.roll(more, shift, 1)
            vectors = more if vectors is None else vectors + more
        vec_ref[...] = vectors
        wait_all(weights)

    x = x_ref[...]
    cols = pl.ds(pl.multiple_of(group * width, 128), width)
    for index, out in enumerate((q_ref, k_ref, v_ref)):
        part = w_ref[:, pl.ds(pl.multiple_of(index * total_width + group * width, 128), width)]
        value = dot(x, part) * scale_ref[index]
        if index != 1:
            value = value + vec_ref[index // 2 : index // 2 + 1, cols]
        out[...] = value.astype(bf16)
    lane = lax.broadcasted_iota(jnp.int32, (1, 128), 1)

    def run(span):
        step = min(block, span)
        for pair in range(width // 128):
            cols = pl.ds(pair * 128, 128)
            for start in range(0, rows, step):
                low = start // span * span
                q_rows = q_ref[start : start + step, cols]
                k_rows = k_ref[low : low + span, cols]
                v_rows = v_ref[low : low + span, cols]
                found = []
                for head in range(2):
                    own = (lane < 64) if head == 0 else (lane >= 64)
                    q_own = jnp.where(own, q_rows, jnp.zeros_like(q_rows)) * jnp.asarray(0.125, bf16)
                    v_ones = jnp.where(own, v_rows, jnp.ones_like(v_rows))
                    scores = dot_last(q_own, k_rows)
                    top = jnp.max(scores, axis=1, keepdims=True)
                    found.append((dot(jnp.exp(scores - top).astype(bf16), v_ones), top))
                (out_a, top_a), (out_b, top_b) = found
                value = jnp.where(lane < 64, out_a, out_b)
                total = jnp.where(lane < 64, pltpu.roll(out_a, 64, 1), pltpu.roll(out_b, 64, 1))
                c_ref[start : start + step, cols] = (value / total).astype(bf16)
                lse_ref[start : start + step, cols] = jnp.where(lane < 64, top_a, top_b) + jnp.log(total)

    two = len_ref[0] < rows

    @pl.when(two)
    def _():
        run(rows // 2)

    @pl.when(jnp.logical_not(two))
    def _():
        run(rows)


def attn_fwd(place, lengths, scales, pieces, x, deps):
    rows, width = x.shape
    group = 256
    count = len(pieces)
    cols = pl.BlockSpec((rows, group), lambda g: (0, g))
    return pl.pallas_call(
        functools.partial(attn_fwd_kernel, block=512, count=count, deps=len(deps)),
        grid=(width // group,),
        in_specs=[SMEM] * 3 + [ANY] * (count + len(deps)) + [pl.BlockSpec((rows, width), lambda g: (0, 0))],
        out_specs=[cols] * 5 + [pl.BlockSpec((16, width), lambda g: (0, 0))],
        out_shape=[SDS((rows, width), bf16)] * 4 + [SDS((rows, width), f32), SDS((16, width), f32)],
        scratch_shapes=[pltpu.VMEM((width, 3 * width), bf16), pltpu.VMEM((count, 16, width), bf16),
                        pltpu.SemaphoreType.DMA((3 * count,)), pltpu.SemaphoreType.DMA((count,))],
        compiler_params=params(),
        cost_estimate=cost(20e9, 12e6, 12e6),
        name="attention_forward",
    )(place, lengths, scales, *pieces, *deps, x)


def order_rows(place_ref, source_t, dest):
    cores = dest.shape[0]
    if cores == 1:
        dest[0] = source_t
        return
    blocks = 8
    size = source_t.shape[0] // blocks
    for block in range(blocks):
        at = pl.multiple_of(((block // 2) ^ place_ref[1]) * size, 16)
        dest[(block % 2) ^ place_ref[0], pl.ds(at, size), :] = source_t[block * size : (block + 1) * size]


def turn_kernel(place_ref, source_ref, out_ref):
    order_rows(place_ref, source_ref[...].T, out_ref)


def turn(place, source, cores):
    rows, width = source.shape
    vmem = pl.BlockSpec(memory_space=pltpu.VMEM)
    return pl.pallas_call(
        turn_kernel,
        in_specs=[SMEM, vmem],
        out_specs=vmem,
        out_shape=SDS((cores, width // cores, rows), bf16),
        compiler_params=params(),
        cost_estimate=cost(1e6, 3e6),
        name="turn",
    )(place, source)


def attn_bwd_kernel(
    place_ref, len_ref, q_ref, k_ref, v_ref, dc_ref, c_ref, lse_ref, x_hbm, c_hbm, dh_ref, *refs, block, cores, last, shard_first, deps,
):
    refs = refs[deps:]
    if last:
        before_a_ref, before_b_ref, vg_ref, b1g_ref, *refs = refs
    grads = refs[:cores]
    dqkv_ref, sum_ref, dk_acc, dv_acc, dq_acc, x_t, c_t, sems = refs[cores:]
    rows = q_ref.shape[0]
    pair = pl.program_id(0)
    pairs = pl.num_programs(0)
    span_cols = dqkv_ref.shape[1] // 3
    total_width = x_t.shape[0] * x_t.shape[1]
    lane = lax.broadcasted_iota(jnp.int32, (1, 128), 1)
    masks = [lane < 64, lane >= 64]

    turned_copies = [
        pltpu.make_async_copy(x_hbm, x_t, sems.at[0]),
        pltpu.make_async_copy(c_hbm, c_t, sems.at[1]),
    ]

    @pl.when(pair == 0)
    def _():
        for copy in turned_copies:
            copy.start()

    prod = (dc_ref[...].astype(f32) * c_ref[...].astype(f32)).T
    row_dots = [col_sum(prod[:64]), col_sum(prod[64:])]
    lse = lse_ref[...].T
    lse_rows = [lse[0:1], lse[64:65]]

    def run(span):
        step = min(block, span)
        for low in range(0, rows, span):
            k_rows = k_ref[low : low + span, :]
            v_rows = v_ref[low : low + span, :]
            k_cols = k_rows.astype(f32).T.astype(bf16)
            for start in range(low, low + span, step):
                q_rows = q_ref[start : start + step, :]
                dc_rows = dc_ref[start : start + step, :]
                probs, d_scores, q_own, dc_own, dq_parts = [], [], [], [], []
                for head in range(2):
                    q_head = jnp.where(masks[head], q_rows, jnp.zeros_like(q_rows)) * jnp.asarray(0.125, bf16)
                    dc_head = jnp.where(masks[head], dc_rows, jnp.zeros_like(dc_rows))
                    prob = jnp.exp(dot_last(k_rows, q_head) - lse_rows[head][:, start : start + step])
                    d_prob = dot_last(v_rows, dc_head)
                    d_score = (prob * (d_prob - row_dots[head][:, start : start + step])).astype(bf16)
                    probs.append(prob.astype(bf16))
                    d_scores.append(d_score)
                    q_own.append(q_head)
                    dc_own.append(dc_head)
                    dq_parts.append(dot(k_cols[head * 64 : head * 64 + 64], d_score))
                dq_acc[:, start : start + step] = jnp.concatenate(dq_parts, axis=0)
                dv = dot(jnp.concatenate(probs, axis=1), jnp.concatenate(dc_own, axis=0))
                dk = dot(jnp.concatenate(d_scores, axis=1), jnp.concatenate(q_own, axis=0))
                if start == low:
                    dv_acc[low : low + span, :] = dv
                    dk_acc[low : low + span, :] = dk
                else:
                    dv_acc[low : low + span, :] += dv
                    dk_acc[low : low + span, :] += dk

    two = len_ref[0] < rows

    @pl.when(two)
    def _():
        run(rows // 2)

    @pl.when(jnp.logical_not(two))
    def _():
        run(rows)

    dq = dq_acc[...].T * 0.125

    def put(part, value):
        at = pl.multiple_of(part * span_cols + pair * 128, 128)
        dqkv_ref[:, pl.ds(at, 128)] = value.astype(bf16)

    put(0, dq)
    put(1, dk_acc[...])
    put(2, dv_acc[...])
    low = before_a_ref.shape[1] if last else 0
    here = pl.ds(pl.multiple_of(low + pair * 128, 128), 128)
    if last:
        @pl.when(pair == 0)
        def _():
            sum_ref[0:2, : before_a_ref.shape[1]] = before_a_ref[0:2, :]
            sum_ref[0:2, low + span_cols :] = before_b_ref[0:2, :]
            sum_ref[2:8, :] = vg_ref[2:8, :]
            for row in range(b1g_ref.shape[1] // total_width):
                sum_ref[8 + row : 9 + row, :] = b1g_ref[0:1, row * total_width : (row + 1) * total_width]

    sum_ref[0:1, here] = col_sum(dq)
    sum_ref[1:2, here] = col_sum(dv_acc[...])

    @pl.when(pair == pairs - 1)
    def _():
        for copy in turned_copies:
            copy.wait()
        for core in reversed(range(cores)):
            out = grads[core]
            spots = out.shape[1 if shard_first else 0]
            size = x_t.shape[1] // spots
            for plane in range(4):
                left = x_t if plane < 3 else c_t
                right = dqkv_ref[:, plane * span_cols : (plane + 1) * span_cols] if plane < 3 else dh_ref[...]
                value = dot(left[core], right).astype(bf16)
                if shard_first:
                    out[plane] = value.reshape(spots, size, span_cols)
                else:
                    out[:, pl.ds(plane ^ place_ref[2], 1), :size] = value.reshape(spots, 1, size, span_cols)
        if last and cores == 2:
            row = lax.broadcasted_iota(jnp.int32, (16, span_cols), 0)
            col = lax.broadcasted_iota(jnp.int32, (16, span_cols), 1)
            kept = (row < 3) & (col < size)
            even = place_ref[0] == 0
            for plane in range(4):
                rows_here = sum_ref[...] if plane == 0 else pltpu.roll(sum_ref[...], 16 - 3 * plane, 0)
                for spot in range(4):
                    tiles = []
                    for core in range(2):
                        start = (2 * spot + core) * size
                        turned = rows_here if start == 0 else pltpu.roll(rows_here, total_width - start, 1)
                        tiles.append(jnp.where(kept, turned[:, :span_cols], 0.0).astype(bf16))
                    for core in range(2):
                        tile = jnp.where(even, tiles[core], tiles[1 - core])
                        grads[core][spot ^ place_ref[1], plane ^ place_ref[2], size:, :] = tile


def attn_bwd(place, lengths, q, k, v, dc, c, lse, x_turned, c_turned, dh_low, first, pairs, cores, spots, deps, before=None, shard_first=False):
    rows, width = q.shape
    last = before is not None
    size = pairs * 128
    cols = pl.BlockSpec((rows, 128), lambda g: (0, first + g))

    def whole(shape):
        return pl.BlockSpec(shape, lambda g: (0,) * len(shape))

    depth = width // (cores * spots)
    shape = (spots, 4, depth + (16 if last and cores == 2 else 0), size)
    shape = (shape[1], shape[0]) + shape[2:] if shard_first else shape
    sums = (16, width if last else size)
    more = list(before) if last else []
    return pl.pallas_call(
        functools.partial(attn_bwd_kernel, block=512, cores=cores, last=last, shard_first=shard_first, deps=len(deps)),
        grid=(pairs,),
        in_specs=[SMEM] * 2 + [cols] * 6 + [ANY] * 2
        + [pl.BlockSpec((rows, size), lambda g: (0, first // pairs))] + [ANY] * len(deps) + [whole(m.shape) for m in more],
        out_specs=[whole(shape)] * cores + [whole((rows, 3 * size)), whole(sums)],
        out_shape=[SDS(shape, bf16)] * cores + [SDS((rows, 3 * size), bf16), SDS(sums, f32)],
        scratch_shapes=[
            pltpu.VMEM((rows, 128), f32), pltpu.VMEM((rows, 128), f32), pltpu.VMEM((128, rows), f32),
            pltpu.VMEM((cores, width // cores, rows), bf16), pltpu.VMEM((cores, width // cores, rows), bf16),
            pltpu.SemaphoreType.DMA((2,)),
        ],
        compiler_params=params(),
        cost_estimate=cost(50e9 * size / width, 30e6 * size / width, 12e6 * size / width),
        name="attention_backward",
    )(place, lengths, q, k, v, dc, c, lse, x_turned, c_turned, dh_low, *deps, *more)


def mid_fwd_kernel(place_ref, scale_ref, *refs, chunk, count, deps):
    pieces = refs[:count]
    refs = refs[:count] + refs[count + deps :]
    (x_ref, c_ref, vec_ref, n1_ref, r1_ref, y1_ref, a_ref, gp_ref,
     wo_ref, w1_ref, out_sems, up_sems) = refs[count:]
    rows, width = x_ref.shape
    first = pl.program_id(0) == 0
    out_copies = block_copies(place_ref, pieces, [4], wo_ref, out_sems)
    up_copies = block_copies(place_ref, pieces, range(4), w1_ref, up_sems)

    @pl.when(first)
    def _():
        start_all(out_copies)
        start_all(up_copies)
        wait_all(out_copies)

    residual = x_ref[...].astype(f32) + dot(c_ref[...], wo_ref[...]) * scale_ref[3] + vec_ref[2:3]
    normed, inv_std = normalize(residual)
    n1_ref[...] = normed
    r1_ref[...] = jnp.broadcast_to(inv_std, (rows, 128))
    y1 = (normed * vec_ref[3:4] + vec_ref[4:5]).astype(bf16)
    y1_ref[...] = y1

    @pl.when(first)
    def _():
        wait_all(up_copies)

    for start in range(0, w1_ref.shape[1], chunk):
        block, at = divmod(start, width)
        cols = slice(start, start + chunk)
        bias = vec_ref[8 + block : 9 + block, at : at + chunk]
        u = dot(y1, w1_ref[:, cols]) * scale_ref[4] + bias
        square = u * u
        half = 0.5 + 0.5 * jnp.tanh(u * (GELU_K + (GELU_K * GELU_C) * square))
        act = u * half
        a_ref[:, cols] = act.astype(bf16)
        gp_ref[:, cols] = (half + act * (1.0 - half) * (2 * GELU_K + (6 * GELU_K * GELU_C) * square)).astype(bf16)


def mid_fwd(place, scales, pieces, x, c, vec, deps):
    rows, width = x.shape
    hidden = 4 * pieces[0].shape[1]
    tile = 512
    count = len(pieces)

    def row(size):
        return pl.BlockSpec((tile, size), lambda i: (i, 0))

    def full(arr):
        return pl.BlockSpec(arr.shape, lambda i: (0, 0))

    return pl.pallas_call(
        functools.partial(mid_fwd_kernel, chunk=256, count=count, deps=len(deps)),
        grid=(rows // tile,),
        in_specs=[SMEM] * 2 + [ANY] * (count + len(deps)) + [row(width), row(width), full(vec)],
        out_specs=[row(width), row(128), row(width), row(hidden), row(hidden)],
        out_shape=[SDS((rows, width), f32), SDS((rows, 128), f32), SDS((rows, width), bf16),
                   SDS((rows, hidden), bf16), SDS((rows, hidden), bf16)],
        scratch_shapes=[pltpu.VMEM((width, width), bf16), pltpu.VMEM((width, hidden), bf16),
                        pltpu.SemaphoreType.DMA((count,)), pltpu.SemaphoreType.DMA((4 * count,))],
        compiler_params=params(),
        cost_estimate=cost(12e9, 25e6, 3e6),
        name="middle_forward",
    )(place, scales, *pieces, *deps, x, c, vec)


def second_norm_kernel(place_ref, scale_ref, *refs, cores, tiles):
    downs = refs[:cores]
    (act_ref, n1_ref, do_ref, vec_ref, out_ref, dz_ref, dzb_ref, vg_ref, grad_ref,
     w2_ref, act, dz_all, left_t, down_sems, act_sems) = refs[cores:]
    step = pl.program_id(0)
    tile = n1_ref.shape[0]

    def act_copy(index):
        rows = pl.ds(pl.multiple_of(index * tile, tile), tile)
        return pltpu.make_async_copy(act_ref.at[rows], act.at[rows], act_sems.at[index])

    copies = down_copies(place_ref, downs, w2_ref, down_sems)
    spots = downs[0].shape[1]
    size = w2_ref.shape[1] // spots

    def body(arriving):
        if arriving:
            act_copy(0).start()
            start_all(copies)
            for index in range(1, tiles):
                act_copy(index).start()
            vg_ref[...] = jnp.zeros_like(vg_ref)
        act_copy(step).wait()
        rows = pl.ds(pl.multiple_of(step * tile, tile), tile)
        g1, c1, b2, g2, c2 = [vec_ref[i : i + 1] for i in range(3, 8)]
        if arriving:
            product = None
            for spot in range(spots):
                wait_all(some_copies(copies, spot, spots))
                cols = slice(spot * size, (spot + 1) * size)
                more = dot_last(act[rows, cols], w2_ref[:, cols])
                product = more if product is None else product + more
        else:
            product = dot_last(act[rows, :], w2_ref[...])
        residual = n1_ref[...] * g1 + c1 + product * scale_ref[5] + b2
        n2, r2 = normalize(residual)
        out_ref[...] = (n2 * g2 + c2).astype(bf16)
        d_out = do_ref[...].astype(f32)
        vg_ref[6:7] += col_sum(d_out * n2)
        vg_ref[7:8] += col_sum(d_out)
        dz = normalize_back(d_out * g2, n2, r2)
        vg_ref[5:6] += col_sum(dz)
        dz_ref[...] = dz
        dz_low = dz.astype(bf16)
        dzb_ref[...] = dz_low
        dz_all[rows, :] = dz_low

    @pl.when(step == 0)
    def _():
        body(True)

    @pl.when((step > 0) & (step < tiles))
    def _():
        body(False)

    @pl.when(step == tiles)
    def _():
        left_t[...] = dz_all[...].T

    @pl.when(step >= tiles)
    def _():
        blocks, slots, size, cols = grad_ref.shape
        wide = blocks * cols
        start = pl.multiple_of((step - tiles) * wide, 128)
        value = dot(left_t[...], act[:, pl.ds(start, wide)]).astype(bf16)
        for block in range(blocks):
            grad_ref[block] = value[:, block * cols : (block + 1) * cols].reshape(slots, size, cols)


def second_norm(place, scales, downs, n1, act, d_out, vec, blocks):
    rows, width = n1.shape
    hidden = act.shape[1]
    tile = 256
    tiles = rows // tile
    some = min(2, blocks)
    block = (some, 4, width // 4, hidden // blocks)

    def row(size):
        return pl.BlockSpec((tile, size), lambda i: (jnp.minimum(i, tiles - 1), 0))

    return pl.pallas_call(
        functools.partial(second_norm_kernel, cores=len(downs), tiles=tiles),
        grid=(tiles + blocks // some,),
        in_specs=[SMEM] * 2 + [ANY] * (len(downs) + 1)
        + [row(width), row(width), pl.BlockSpec(vec.shape, lambda i: (0, 0))],
        out_specs=[row(width)] * 3 + [pl.BlockSpec((8, width), lambda i: (0, 0)),
                                      pl.BlockSpec(block, lambda i: (jnp.maximum(i - tiles, 0), 0, 0, 0))],
        out_shape=[SDS((rows, width), bf16), SDS((rows, width), f32), SDS((rows, width), bf16), SDS((8, width), f32),
                   SDS((blocks,) + block[1:], bf16)],
        scratch_shapes=[pltpu.VMEM((width, hidden), bf16), pltpu.VMEM((rows, hidden), bf16),
                        pltpu.VMEM((rows, width), bf16), pltpu.VMEM((width, rows), bf16),
                        pltpu.SemaphoreType.DMA((4 * downs[0].shape[1] * len(downs),)),
                        pltpu.SemaphoreType.DMA((tiles,))],
        compiler_params=params(),
        cost_estimate=cost(16e9, 30e6),
        name="second_norm",
    )(place, scales, *downs, act, n1, d_out, vec)


def mid_bwd_kernel(place_ref, scale_ref, *refs, chunk, count, cores, outs, tiles, deps):
    downs, pieces, refs = refs[:cores], refs[cores : cores + count], refs[cores + count + deps :]
    y1_hbm, n1_ref, r1_ref, gp_ref, dz_ref, dzb_ref, vec_ref = refs[:7]
    dh_ref, dhb_ref, dc_ref, vg_ref, b1g_ref = refs[7:12]
    grads = refs[12 : 12 + outs]
    wo_ref, w1_ref, w2_ref, du_all, y1, left_t, out_sems, up_sems, down_sems, y1_sem = refs[12 + outs :]
    step = pl.program_id(0)
    tile, width = n1_ref.shape
    first = step == 0
    y1_copy = pltpu.make_async_copy(y1_hbm, y1, y1_sem.at[0])

    w2_copies = down_copies(place_ref, downs, w2_ref, down_sems)
    w1_copies = block_copies(place_ref, pieces, range(4), w1_ref, up_sems)
    wo_copies = block_copies(place_ref, pieces, [4], wo_ref, out_sems)
    spots = downs[0].shape[1]

    def body(arriving):
        if arriving:
            start_all(w2_copies)
            start_all(w1_copies)
            start_all(wo_copies)
            y1_copy.start()
            vg_ref[...] = jnp.zeros_like(vg_ref)
            b1g_ref[...] = jnp.zeros_like(b1g_ref)
        rows = pl.ds(pl.multiple_of(step * tile, tile), tile)
        g1 = vec_ref[3:4]
        n1 = n1_ref[...]
        dz_low = dzb_ref[...]
        for start in range(0, w1_ref.shape[1], chunk):
            spot, rest = divmod(start * spots, w1_ref.shape[1])
            if arriving and rest == 0:
                wait_all(some_copies(w2_copies, spot, spots))
            cols = slice(start, start + chunk)
            du = dot(dz_low, w2_ref[:, cols]) * scale_ref[5] * gp_ref[:, cols].astype(f32)
            b1g_ref[0:1, cols] += col_sum(du)
            du_all[rows, cols] = du.astype(bf16)
        if arriving:
            wait_all(w1_copies)
            wait_all(wo_copies)
        dy = dz_ref[...] + dot_last(du_all[rows, :], w1_ref[...]) * scale_ref[4]
        vg_ref[3:4] += col_sum(dy * n1)
        vg_ref[4:5] += col_sum(dy)
        dh = normalize_back(dy * g1, n1, r1_ref[:, 0:1])
        vg_ref[2:3] += col_sum(dh)
        dh_ref[...] = dh
        dh_low = dh.astype(bf16)
        dhb_ref[...] = dh_low
        dc_ref[...] = (dot_last(dh_low, wo_ref[...]) * scale_ref[3]).astype(bf16)

    @pl.when(first)
    def _():
        body(True)

    @pl.when((step > 0) & (step < tiles))
    def _():
        body(False)

    @pl.when(step == tiles)
    def _():
        y1_copy.wait()
        order_rows(place_ref, y1[...].T, left_t)

    @pl.when(step >= tiles)
    def _():
        cols = pl.ds(pl.multiple_of((step - tiles) * width, 128), width)
        for core in reversed(range(outs)):
            grads[core][...] = dot(left_t[core], du_all[:, cols]).astype(bf16).reshape(grads[core].shape)


def mid_bwd(place, scales, pieces, downs, n1, r1, y1, gelu_grad, dz, dz_low, vec, cores, spots, deps):
    rows, width = n1.shape
    hidden = gelu_grad.shape[1]
    tile = 256
    tiles = rows // tile
    count = len(pieces)
    block = (spots, 1, width // (cores * spots), width)

    def row(size):
        return pl.BlockSpec((tile, size), lambda i: (jnp.minimum(i, tiles - 1), 0))

    def whole(shape):
        return pl.BlockSpec(shape, lambda i: (0,) * len(shape))

    return pl.pallas_call(
        functools.partial(
            mid_bwd_kernel, chunk=256, count=count, cores=len(downs), outs=cores, tiles=tiles, deps=len(deps)
        ),
        grid=(tiles + 4,),
        in_specs=[SMEM] * 2 + [ANY] * (count + len(downs) + len(deps) + 1)
        + [row(width), row(128), row(hidden), row(width), row(width), whole(vec.shape)],
        out_specs=[row(width), row(width), row(width), whole((8, width)), whole((8, hidden))]
        + [pl.BlockSpec(block, lambda i: (0, jnp.maximum(i - tiles, 0), 0, 0))] * cores,
        out_shape=[SDS((rows, width), f32), SDS((rows, width), bf16), SDS((rows, width), bf16),
                   SDS((8, width), f32), SDS((8, hidden), f32)]
        + [SDS((spots, 4) + block[2:], bf16)] * cores,
        scratch_shapes=[pltpu.VMEM((width, width), bf16), pltpu.VMEM((width, hidden), bf16),
                        pltpu.VMEM((width, hidden), bf16), pltpu.VMEM((rows, hidden), bf16),
                        pltpu.VMEM((rows, width), bf16), pltpu.VMEM((cores, width // cores, rows), bf16),
                        pltpu.SemaphoreType.DMA((count,)), pltpu.SemaphoreType.DMA((4 * count,)),
                        pltpu.SemaphoreType.DMA((4 * downs[0].shape[1] * len(downs),)),
                        pltpu.SemaphoreType.DMA((1,))],
        compiler_params=params(),
        cost_estimate=cost(28e9, 40e6),
        name="middle_backward",
    )(place, scales, *downs, *pieces, *deps, y1, n1, r1, gelu_grad, dz, dz_low, vec)


def input_grad_kernel(place_ref, scale_ref, *refs, count, chunks, deps):
    pieces = refs[:count]
    parts = refs[count : count + chunks]
    dh_ref, out_ref, w_ref, sems = refs[count + chunks + deps :]
    width = dh_ref.shape[1]

    @pl.when(pl.program_id(0) == 0)
    def _():
        copies = block_copies(place_ref, pieces, range(3), w_ref, sems)
        start_all(copies)
        wait_all(copies)

    total = dh_ref[...]
    for plane in range(3):
        product = None
        start = plane * width
        for part in parts:
            size = part.shape[1] // 3
            more = dot_last(part[:, plane * size : (plane + 1) * size], w_ref[:, start : start + size])
            product = more if product is None else product + more
            start += size
        total = total + product * scale_ref[plane]
    out_ref[...] = total.astype(bf16)


def input_grad(place, scales, pieces, parts, dh, deps):
    rows, width = dh.shape
    tile = 512
    count, chunks = len(pieces), len(parts)

    def row(size):
        return pl.BlockSpec((tile, size), lambda i: (i, 0))

    return pl.pallas_call(
        functools.partial(input_grad_kernel, count=count, chunks=chunks, deps=len(deps)),
        grid=(rows // tile,),
        in_specs=[SMEM] * 2 + [ANY] * count + [row(p.shape[1]) for p in parts] + [ANY] * len(deps) + [row(width)],
        out_specs=row(width),
        out_shape=SDS((rows, width), bf16),
        scratch_shapes=[pltpu.VMEM((width, 3 * width), bf16), pltpu.SemaphoreType.DMA((3 * count,))],
        compiler_params=params(),
        cost_estimate=cost(9e9, 2 * (rows * width * 6 + 3 * width * width)),
        name="input_gradient",
    )(place, scales, *pieces, *parts, *deps, dh)


def swap(value, axis, mask):
    count = lax.axis_size(axis)
    return lax.ppermute(value, axis, [(i, i ^ mask) for i in range(count)])


def bits(axis):
    return [1 << b for b in range(lax.axis_size(axis).bit_length() - 1)]


def doubling_gather(value, axis, dim):
    index = lax.axis_index(axis)
    for bit in bits(axis):
        other = swap(value, axis, bit)
        high = (index & bit) != 0
        value = jnp.concatenate(
            [jnp.where(high, other, value), jnp.where(high, value, other)], axis=dim
        )
    return value


def doubling_sum(value):
    for axis in ("dp", "shard"):
        for bit in bits(axis):
            value = value + swap(value, axis, bit)
    return value


def total_sum(value):
    value = value + swap(value, "dp", 1)
    for axis, masks in (("dp", (6, 4, 2)), ("shard", (3, 2, 1))):
        others = [swap(value, axis, mask) for mask in masks]
        value = (value + others[0]) + (others[1] + others[2])
    return value


def four(block, axis, unit):
    return [block] + [swap(block, axis, unit * m) for m in (1, 2, 3)]


def core_sum_kernel(*refs, sizes, deps):
    count = len(sizes)
    outs = refs[2 * count + deps :]
    at = 0
    for index, (depth, width) in enumerate(sizes):
        mine, got = refs[2 * index : 2 * index + 2]
        for spot, out in enumerate(outs):
            total = mine[spot, 0].astype(f32) + got[spot, 0].astype(f32)
            out[0, :depth, at : at + width] = total.astype(bf16)
            if depth < out.shape[1]:
                out[0, depth:, at : at + width] = jnp.zeros((out.shape[1] - depth, width), bf16)
        at += width


def core_sum(pairs, deps=()):
    spots, slots = pairs[0][0].shape[:2]
    sizes = [mine.shape[2:] for mine, _ in pairs]
    rows, width = max(s[0] for s in sizes), sum(s[1] for s in sizes)
    specs = []
    for mine, got in pairs:
        specs += [pl.BlockSpec((spots, 1) + mine.shape[2:], lambda i: (0, i, 0, 0))] * 2
    return pl.pallas_call(
        functools.partial(core_sum_kernel, sizes=sizes, deps=len(deps)),
        grid=(slots,),
        in_specs=specs + [ANY] * len(deps),
        out_specs=[pl.BlockSpec((1, rows, width), lambda i: (i, 0, 0))] * spots,
        out_shape=[SDS((slots, rows, width), bf16)] * spots,
        compiler_params=params(),
        cost_estimate=cost(1e6, 6 * spots * slots * rows * width),
        name="core_sum",
    )(*[part for pair in pairs for part in pair], *deps)


def pair_sum_kernel(mine_ref, got_ref, *refs):
    refs[-1][...] = (mine_ref[...].astype(f32) + got_ref[...].astype(f32)).astype(bf16)


def pair_sum(mine, got, deps=()):
    block = pl.BlockSpec((1,) + mine.shape[1:], lambda i: (i, 0, 0, 0))
    return pl.pallas_call(
        pair_sum_kernel,
        grid=mine.shape[:1],
        in_specs=[block, block] + [ANY] * len(deps),
        out_specs=block,
        out_shape=SDS(mine.shape, bf16),
        compiler_params=params(),
        cost_estimate=cost(1e6, 6 * mine.size),
        name="pair_sum",
    )(mine, got, *deps)


def plane_sum_kernel(*refs, count, deps):
    outs = refs[4 * count + deps :]
    at = 0
    for index in range(count):
        parts = refs[4 * index : 4 * index + 4]
        depth, width = parts[0].shape[1:]
        for slot in range(parts[0].shape[0]):
            total = parts[0][slot].astype(f32) + parts[1][slot].astype(f32)
            total = total + (parts[2][slot].astype(f32) + parts[3][slot].astype(f32))
            out = outs[0].at[slot] if len(outs) == 1 else outs[slot]
            out[:depth, at : at + width] = total.astype(out.dtype)
            if depth < out.shape[0]:
                out[depth:, at : at + width] = jnp.zeros((out.shape[0] - depth, width), out.dtype)
        at += width


def plane_sum(groups, split, deps=()):
    slots = groups[0][0].shape[0]
    rows = max(parts[0].shape[1] for parts in groups)
    width = sum(parts[0].shape[2] for parts in groups)
    vmem = pl.BlockSpec(memory_space=pltpu.VMEM)
    shapes = [SDS((rows, width), f32)] + [SDS((rows, width), bf16)] * (slots - 1)
    if not split:
        shapes = [SDS((slots, rows, width), bf16)]
    return pl.pallas_call(
        functools.partial(plane_sum_kernel, count=len(groups), deps=len(deps)),
        in_specs=[vmem] * (4 * len(groups)) + [ANY] * len(deps),
        out_specs=[vmem] * len(shapes),
        out_shape=shapes,
        compiler_params=params(),
        cost_estimate=cost(1e6, 4 * slots * rows * width),
        name="plane_sum",
    )(*[part for parts in groups for part in parts], *deps)


def exchange(parts, axis, unit):
    return [parts[0]] + [swap(parts[m], axis, unit * m) for m in (1, 2, 3)]


def after(value, *others):
    return lax.optimization_barrier((value,) + others)[0]

def adam_update(gradient, master, first_old, second_old, average, step_rate, decay_rate):
    first_new = beta_first * first_old + (1.0 - beta_first) * gradient
    second_new = beta_second * second_old + (1.0 - beta_second) * gradient * gradient
    first_hat = first_new / (1.0 - beta_first**STEP)
    second_hat = second_new / (1.0 - beta_second**STEP)
    master_new = master - step_rate * (
        first_hat / (jnp.sqrt(second_hat) + adam_eps) + decay_rate * master
    )
    average_new = average_keep * average + (1.0 - average_keep) * master_new
    return (first_new, second_new, master_new, average_new)


def own_sums_kernel(*refs):
    firsts, lasts, (up_ref, down_ref, attn_ref, vec_ref, square_ref) = refs[:4], refs[4:8], refs[8:]
    rows = attn_ref.shape[0]
    first, last = [
        (parts[0][...].astype(f32) + parts[1][...].astype(f32)) + (parts[2][...].astype(f32) + parts[3][...].astype(f32))
        for parts in (firsts, lasts)
    ]
    attn_ref[:, : first.shape[1]] = first
    attn_ref[:, first.shape[1] :] = last[:rows]
    at = 0
    vec_ref[...] = last[rows:, at : at + 128]
    total = jnp.sum(first * first) + jnp.sum(last * last)
    for ref in (up_ref, down_ref):
        value = ref[...].astype(f32)
        total = total + jnp.sum(value * value)
    square_ref[...] = jnp.full(square_ref.shape, total, f32)


def own_sums(firsts, lasts, own_up, own_down):
    vmem = pl.BlockSpec(memory_space=pltpu.VMEM)
    rows, width = firsts[0].shape[0], firsts[0].shape[1] + lasts[0].shape[1]
    return pl.pallas_call(
        own_sums_kernel,
        in_specs=[vmem] * 10,
        out_specs=[vmem] * 3,
        out_shape=[SDS((rows, width), f32), SDS((16, 128), f32), SDS((8, 128), f32)],
        compiler_params=params(),
        cost_estimate=cost(1e6, 2e6),
        name="own_sums",
    )(*firsts, *lasts, own_up, own_down)


def update_kernel(square_ref, attn_ref, up_ref, down_ref, vec_ref, *refs):
    states, news, norm_ref = refs[:16], refs[16:32], refs[32]
    norm = jnp.sqrt(square_ref[...])
    norm_ref[0, 0] = jnp.max(norm)
    factor = jnp.minimum(1.0, clip_limit / (norm + norm_eps))[0:1, 0:1]
    rows, cols = states[12].shape
    grads = (
        attn_ref[...],
        up_ref[...].astype(f32),
        down_ref[...].astype(f32),
        vec_ref[:rows, :cols],
    )
    for index, grad in enumerate(grads):
        rates = (vector_rate, 0.0) if index == 3 else (matrix_rate, matrix_decay)
        old = [ref[...] for ref in states[4 * index : 4 * index + 4]]
        for ref, new in zip(news[4 * index : 4 * index + 4], adam_update(grad * factor, *old, *rates)):
            ref[...] = new


def update(squares, own_attn, own_up, own_down, own_vector, states):
    vmem = pl.BlockSpec(memory_space=pltpu.VMEM)
    states = list(states[:8]) + [state.T for state in states[8:]]
    *news, norm = pl.pallas_call(
        update_kernel,
        in_specs=[vmem] * 21,
        out_specs=[vmem] * 16 + [SMEM],
        out_shape=[SDS(state.shape, f32) for state in states] + [SDS((1, 1), f32)],
        compiler_params=params(),
        cost_estimate=cost(1e7, 8e6),
        name="state_update",
    )(squares, own_attn, own_up, own_down, own_vector, *states)
    return news[:8] + [new.T for new in news[8:]], norm


def on_device(
    tokens, out_grad, first_lengths, quant_scales, attn_quant, up_quant, down_quant,
    attn_master, attn_first, attn_second, attn_average,
    up_master, up_first, up_second, up_average,
    down_master, down_first, down_second, down_average,
    vector_master, vector_first, vector_second, vector_average,
):
    width = tokens.shape[1]
    dp_index, shard_index = lax.axis_index("dp"), lax.axis_index("shard")
    small = lax.axis_size("dp") == 8 and lax.axis_size("shard") == 4 and attn_quant.shape == (96, 768)
    gather = functools.partial(lax.all_gather, tiled=True)
    scatter = functools.partial(lax.psum_scatter, tiled=True)
    down_turned = down_quant.T
    vector_low = vector_master.astype(bf16)
    if small:
        cores, spots = 2, 4
        place = jnp.stack([dp_index & 1, dp_index >> 1, shard_index]).astype(jnp.int32)
        packed = jnp.pad(vector_low.T, ((0, 13), (0, width - 96)))
        blocks = four(jnp.concatenate([attn_quant, packed]), "shard", 1)
        x_turned = turn(place, tokens, cores)
        qkv, w_out = attn_stack(place, blocks, [x_turned])
        pieces = four(qkv, "dp", 2)
        up_blocks = four(after(up_quant, qkv), "shard", 1)
        down = after(lax.all_gather(down_turned, "dp"), pieces[1]).reshape(4, 2, 192, -1)
        down = lax.dynamic_index_in_dim(down, dp_index & 1, 1, keepdims=False)
        half = down
        down = lax.all_gather(after(down, *pieces[1:], *up_blocks), "shard")
        up = stack(place, up_blocks, 2, w_out, deps=pieces[1:2])
        ups = four(up, "dp", 2)
        pieces = pieces + [swap(after(piece, up, half), "dp", 1) for piece in pieces]
        early = [up]
    else:
        cores, spots = 1, 1
        place = jnp.zeros((3,), jnp.int32)
        x_turned = turn(place, tokens, cores)
        vec_w = doubling_gather(doubling_gather(vector_low, "shard", 1), "dp", 0)
        attn_w = gather(gather(attn_quant, "shard", axis=1), "dp", axis=0)
        up_w = gather(gather(up_quant, "shard", axis=1), "dp", axis=0)
        down_w = gather(gather(down_turned, "shard", axis=0), "dp", axis=1)
        planes = [attn_w[:, i * width : (i + 1) * width] for i in range(4)]
        pieces = [jnp.concatenate(planes[:3] + [jnp.pad(vec_w.T, ((0, 4), (0, 0)))])]
        ups = [jnp.concatenate([up_w[:, i * width : (i + 1) * width] for i in range(4)] + planes[3:])]
        downs = [down_w.reshape(4, 1, width // 4, -1)]
        early = []

    q, k, v, c, lse, vec = attn_fwd(place, first_lengths, quant_scales, pieces, tokens, early)
    c_turned = turn(place, c, cores)
    if small:
        ups = [ups[0]] + [after(piece, c_turned) for piece in ups[1:]]
        ups = ups + [swap(piece, "dp", 1) for piece in ups]
    n1, r1, y1, act, gelu_grad = mid_fwd(place, quant_scales, ups, tokens, c, vec, [c_turned])
    if small:
        downs = [down, swap(after(down, act), "dp", 1)]
    layer_out, dz, dz_low, vec_second, grad_down = second_norm(
        place, quant_scales, downs, n1, act, out_grad, vec, cores * spots
    )
    dh, dh_low, dc, vec_first, b1_grad, *up_parts = mid_bwd(
        place, quant_scales, ups, downs, n1, r1, y1, gelu_grad, dz, dz_low, vec, cores, spots, [grad_down]
    )
    vec_grad = jnp.concatenate([vec_first[:5], vec_second[5:]])
    attn = functools.partial(
        attn_bwd, place, first_lengths, q, k, v, dc, c, lse, x_turned, c_turned, dh_low, cores=cores, spots=spots
    )
    if small:
        own_down = lax.psum_scatter(grad_down, "dp", scatter_dimension=0)
        up_got = swap(up_parts[1], "dp", 1)
        *parts_p, d_p, sums_p = attn(first=4, pairs=2, deps=up_parts[1:])
        up_plane = core_sum([(up_parts[0], up_got)], [d_p])
        got_p = swap(after(parts_p[1], up_plane[0]), "dp", 1)
        up_plane = exchange(up_plane, "dp", 2)
        *parts_q, d_q, sums_q = attn(first=0, pairs=3, deps=up_plane[:1], shard_first=True)
        own_down = lax.psum_scatter(own_down, "shard", scatter_dimension=0)
        (up_shards,) = plane_sum([up_plane], False, [d_q, own_down])
        own_up = lax.psum_scatter(up_shards, "shard", scatter_dimension=0)
        got_q = swap(after(parts_q[1], up_shards), "dp", 1)
        *parts_r, d_r, sums = attn(first=3, pairs=1, deps=[up_shards], before=(sums_q, sums_p, vec_grad, b1_grad))
        got_r = swap(parts_r[1], "dp", 1)
        plane_pr = core_sum([(parts_r[0], got_r), (parts_p[0], got_p)], [d_r])
        sum_q = pair_sum(parts_q[0], got_q, [plane_pr[0], own_up])
        plane_pr = exchange(plane_pr, "dp", 2)
        spots_q = lax.psum_scatter(sum_q, "shard", scatter_dimension=0)
        spots_q = exchange(after(spots_q, plane_pr[1]), "dp", 2)
        input_gradient = input_grad(place, quant_scales, pieces, [d_q, d_r, d_p], dh, [plane_pr[0]])
        slots_pr = exchange(plane_sum([plane_pr], True, [input_gradient]), "shard", 1)
    else:
        parts_p, d_p, sums_p = attn(first=4, pairs=2, deps=[])
        parts_q, d_q, sums_q = attn(first=0, pairs=3, deps=[])
        parts_r, d_r, sums = attn(first=3, pairs=1, deps=[], before=(sums_q, sums_p, vec_grad, b1_grad))
        attn_parts = [[parts_q], [parts_r], [parts_p]]
        input_gradient = input_grad(place, quant_scales, pieces, [d_q, d_r, d_p], dh, [])

    rows_own, cols_own = vector_master.shape
    states = (
        attn_master, attn_first, attn_second, attn_average,
        up_master, up_first, up_second, up_average,
        down_master, down_first, down_second, down_average,
        vector_master, vector_first, vector_second, vector_average,
    )
    if small:
        own_attn, own_vector, squares = own_sums(spots_q, slots_pr, own_up, own_down)
        news, grad_norm = update(total_sum(squares), own_attn, own_up, own_down, own_vector, states)
        return (layer_out, input_gradient, grad_norm.reshape(()), *news)
    vec_total = doubling_sum(sums[:12])
    own_vector = lax.dynamic_slice(vec_total, (shard_index * cols_own, dp_index * rows_own), (cols_own, rows_own)).T
    grad_down = grad_down.reshape(width, -1)
    grad_up = up_parts[0][0].transpose(1, 0, 2).reshape(width, -1)
    grad_attn = jnp.concatenate([parts[0][0] for parts in attn_parts], axis=2)
    grad_attn = grad_attn.transpose(1, 0, 2).reshape(width, -1)
    own_down = scatter(scatter(grad_down, "dp", scatter_dimension=1), "shard", scatter_dimension=0).astype(f32).T
    own_up = scatter(scatter(grad_up, "dp", scatter_dimension=0), "shard", scatter_dimension=1).astype(f32)
    own_attn = scatter(scatter(grad_attn, "dp", scatter_dimension=0), "shard", scatter_dimension=1).astype(f32)
    grads = (own_attn, own_up, own_down, own_vector)
    squares = sum(jnp.sum(grad * grad) for grad in grads)
    grad_norm = jnp.sqrt(doubling_sum(jnp.broadcast_to(squares, (8, 128)))[0, 0])
    factor = jnp.minimum(1.0, clip_limit / (grad_norm + norm_eps))
    news = []
    for index, grad in enumerate(grads):
        rates = (vector_rate, 0.0) if index == 3 else (matrix_rate, matrix_decay)
        news += adam_update(grad * factor, *states[4 * index : 4 * index + 4], *rates)
    return (layer_out, input_gradient, grad_norm, *news)


def solution(mesh):
    rows = P(("dp", "shard"), None)
    block = P("dp", "shard")
    in_specs = (rows, rows, P(("dp", "shard")), P()) + (block,) * 19
    out_specs = (rows, rows, P()) + (block,) * 16
    return jax.shard_map(
        on_device, mesh=mesh, in_specs=in_specs, out_specs=out_specs, check_vma=False
    )
```

profile of v0, /device:TPU:0, one launch (start us, length us, event | category | flops | bytes accessed | tf_op | source)
XLA Modules:
  0.0 332.9 jit_solution(16366671425224614443)
XLA Ops:
  8.7 0.9 fusion.1.refs_0_
  9.6 5.1 %collective-permute-start.2 = (bf16[112,768]{1,0:T(8,128)(2,1)S(1)}, bf16[112,768]{1,0:T(8,128)(2,1)S(1)}, u32[]{:S(2)}, u32[]{:S(2)}) collective-permute-start(bf16[112,768]{1,0:T(8,128)(2,1)S(1)} %fusion.1.refs_0_), channel_id=1, source_target_pairs={{0,3},{1,2},{2,1},{3,0},{4,7},{5,6},{6,5},{7,4},{8,11},{9,10},{10,... | collective-permute-start | bytes 516104 | tf_op jit(solution)/shard_map/ppermute | solution.py:789
  15.9 3.1 turn.2.refs_4_.x_hbm
  19.0 1.0 collective-permute-done.2.refs_3_
  20.0 9.3 %collective-permute-done.1.refs_2_ = bf16[112,768]{1,0:T(8,128)(2,1)S(1)} collective-permute-done((bf16[112,768]{1,0:T(8,128)(2,1)S(1)}, bf16[112,768]{1,0:T(8,128)(2,1)S(1)}, u32[]{:S(2)}, u32[]{:S(2)}) %collective-permute-start.1) | collective-permute-done | bytes 172064 | tf_op jit(solution)/shard_map/ppermute | solution.py:789
  30.6 2.1 attention_weight_order.1
  32.7 1.5 collective-permute-start.3
  34.2 1.5 collective-permute-start.5
  36.2 2.5 collective-permute-start.8
  38.7 5.2 %collective-permute-done.8.refs_3_ = bf16[96,768]{1,0:T(8,128)(2,1)S(1)} collective-permute-done((bf16[96,768]{1,0:T(8,128)(2,1)S(1)}, bf16[96,768]{1,0:T(8,128)(2,1)S(1)}, u32[]{:S(2)}, u32[]{:S(2)}) %collective-permute-start.8) | collective-permute-done | bytes 147488 | tf_op jit(solution)/shard_map/ppermute | solution.py:789
  43.9 4.9 %collective-permute-start.6 = (bf16[96,768]{1,0:T(8,128)(2,1)S(1)}, bf16[96,768]{1,0:T(8,128)(2,1)S(1)}, u32[]{:S(2)}, u32[]{:S(2)}) collective-permute-start(bf16[96,768]{1,0:T(8,128)(2,1)S(1)} %copy-done.13), channel_id=1, source_target_pairs={{0,1},{1,0},{2,3},{3,2},{4,5},{5,4},{6,7},{7,6},{8,9},{9,8},{10,11... | collective-permute-start | bytes 442376 | tf_op jit(solution)/shard_map/ppermute | solution.py:789
  48.8 1.2 collective-permute-done.7.refs_2_
  50.0 2.0 collective-permute-done.6.refs_1_
  52.8 2.2 weight_order.1.refs_8_.refs_0_.refs_2_
  54.9 2.0 dynamic-slice_bitcast_fusion
  59.8 1.9 collective-permute-start.15
  61.6 1.1 collective-permute-start.14
  63.5 27.1 %attention_forward.1 = (bf16[1024,768]{1,0:T(8,128)(2,1)}, bf16[1024,768]{1,0:T(8,128)(2,1)}, bf16[1024,768]{1,0:T(8,128)(2,1)}, bf16[1024,768]{1,0:T(8,128)(2,1...) custom-call(s32[3]{0:T(128)} %pad_add_fusion.place_ref, s32[1]{0:T(128)S(6)} %copy.43.len_ref, f32[6]{0:T(128)} %scale_ref.9, ...), custom_call_target="tpu_custom_call" | custom-call | flops 20000000000 | bytes 12000000 | tf_op jit(solution)/shard_map/attention_forward/pallas_call | solution.py:264
  90.6 3.1 turn.3.refs_8_.c_hbm
  93.7 1.4 collective-permute-done.14.refs_2_.refs_4_
  95.7 2.5 collective-permute-done.17.refs_5_.refs_7_
  98.8 1.1 collective-permute-done.19.refs_7_.refs_9_
  99.8 20.9 %middle_forward.1 = (f32[1024,768]{1,0:T(8,128)}, f32[1024,128]{1,0:T(8,128)}, bf16[1024,768]{1,0:T(8,128)(2,1)}, bf16[1024,3072]{1,0:T(8,128)(2,1)}, bf16[1024,3072]{1,0:T(8,128)(2,1)}) custom-call(s32[3]{0:T(128)} %pad_add_fusion.place_ref, f32[6]{0:T(128)} %scale_ref.9, bf16[480,768]{1,0:T(8,128)(2,1)} %weight_order.1.refs_8_.refs_0_.refs_2_, ...), custom_call_target="tpu_custom_call" | custom-call | flops 12000000000 | bytes 25000000 | tf_op jit(solution)/shard_map/middle_forward/pallas_call | solution.py:520
  120.9 4.7 %collective-permute-done.20.refs_1_ = bf16[4,4,192,384]{3,2,1,0:T(8,128)(2,1)} collective-permute-done((bf16[4,4,192,384]{3,2,1,0:T(8,128)(2,1)}, bf16[4,4,192,384]{3,2,1,0:T(8,128)(2,1)}, u32[]{:S(2)}, u32[]{:S(2)}) %collective-permute-start.20) | collective-permute-done | bytes 2359328 | tf_op jit(solution)/shard_map/ppermute | solution.py:789
  125.7 21.6 %second_norm.1 = (bf16[1024,768]{1,0:T(8,128)(2,1)}, f32[1024,768]{1,0:T(8,128)}, bf16[1024,768]{1,0:T(8,128)(2,1)}, f32[8,768]{1,0:T(8,128)}, bf16[8,4,192,384]{3,2,1,0:T(8,128)(2,1)}) custom-call(s32[3]{0:T(128)} %pad_add_fusion.place_ref, f32[6]{0:T(128)} %scale_ref.9, bf16[4,4,192,384]{3,2,1,0:T(8,128)(2,1)} %bitcast.61, ...), custom_call_target="tpu_custom_call" | custom-call | flops 16000000000 | bytes 30000000 | tf_op jit(solution)/shard_map/second_norm/pallas_call | solution.py:615
  147.3 31.1 %middle_backward.1 = (f32[1024,768]{1,0:T(8,128)}, bf16[1024,768]{1,0:T(8,128)(2,1)}, bf16[1024,768]{1,0:T(8,128)(2,1)}, f32[8,768]{1,0:T(8,128)}, f32[8,3072]{1...) custom-call(s32[3]{0:T(128)} %pad_add_fusion.place_ref, f32[6]{0:T(128)} %scale_ref.9, ...), custom_call_target="tpu_custom_call" | custom-call | flops 28000000000 | bytes 40000000 | tf_op jit(solution)/shard_map/middle_backward/pallas_call | solution.py:717
  178.7 1.4 pad_maximum_fusion.refs_3_
  180.0 17.6 %attention_backward.3 = (bf16[4,4,96,256]{3,2,1,0:T(8,128)(2,1)}, bf16[4,4,96,256]{3,2,1,0:T(8,128)(2,1)}, bf16[1024,768]{1,0:T(8,128)(2,1)}, f32[16,256]{1,0:T(8,128)}) custom-call(s32[3]{0:T(128)} %pad_add_fusion.place_ref, s32[1]{0:T(128)S(6)} %copy.43.len_ref, bf16[1024,768]{1,0:T(8,128)(2,1)} %get-tuple-element.119.q_ref, ...), custom_call_target="tpu_custom_call" | custom-call | flops 16666667008 | bytes 10000000 | tf_op jit(solution)/shard_map/attention_backward/pallas_call | solution.py:451
  197.6 4.4 %core_sum.2 = (bf16[4,96,768]{2,1,0:T(8,128)(2,1)}, bf16[4,96,768]{2,1,0:T(8,128)(2,1)}, bf16[4,96,768]{2,1,0:T(8,128)(2,1)}, bf16[4,96,768]{2,1,0:T(8,128)(2,1)}) custom-call(bf16[4,4,96,768]{3,2,1,0:T(8,128)(2,1)} %get-tuple-element.131.refs_0_, bf16[4,4,96,768]{3,2,1,0:T(8,128)(2,1)} %collective-permute-done.21.refs_1_, ...), custom_call_target="tpu_custom_call" | custom-call | flops 1000000 | bytes 7077888 | tf_op jit(solution)/shard_map/core_sum/pallas_call | solution.py:847
  202.0 2.7 collective-permute-start.23
  204.7 0.8 collective-permute-start.24
  205.5 25.8 %attention_backward.4 = (bf16[4,4,96,384]{3,2,1,0:T(8,128)(2,1)}, bf16[4,4,96,384]{3,2,1,0:T(8,128)(2,1)}, bf16[1024,1152]{1,0:T(8,128)(2,1)}, f32[16,384]{1,0:T(8,128)}) custom-call(s32[3]{0:T(128)} %pad_add_fusion.place_ref, s32[1]{0:T(128)S(6)} %copy.43.len_ref, bf16[1024,768]{1,0:T(8,128)(2,1)} %get-tuple-element.119.q_ref, ...), custom_call_target="tpu_custom_call" | custom-call | flops 24999999488 | bytes 15000000 | tf_op jit(solution)/shard_map/attention_backward/pallas_call | solution.py:451
  232.6 2.7 plane_sum.2.refs_0_
  235.8 11.4 %attention_backward.5 = (bf16[4,4,112,128]{3,2,1,0:T(8,128)(2,1)}, bf16[4,4,112,128]{3,2,1,0:T(8,128)(2,1)}, bf16[1024,384]{1,0:T(8,128)(2,1)}, f32[16,768]{1,0:T(8,128)}) custom-call(s32[3]{0:T(128)} %pad_add_fusion.place_ref, s32[1]{0:T(128)S(6)} %copy.43.len_ref, bf16[1024,768]{1,0:T(8,128)(2,1)} %get-tuple-element.119.q_ref, ...), custom_call_target="tpu_custom_call" | custom-call | flops 8333333504 | bytes 5000000 | tf_op jit(solution)/shard_map/attention_backward/pallas_call | solution.py:451
  247.4 2.1 collective-permute-done.25.refs_1_
  249.5 3.8 %core_sum.3 = (bf16[4,112,384]{2,1,0:T(8,128)(2,1)}, bf16[4,112,384]{2,1,0:T(8,128)(2,1)}, bf16[4,112,384]{2,1,0:T(8,128)(2,1)}, bf16[4,112,384]{2,1,0:T(8,128)(2,1)}) custom-call(bf16[4,4,112,128]{3,2,1,0:T(8,128)(2,1)} %get-tuple-element.145.refs_0_, bf16[4,4,112,128]{3,2,1,0:T(8,128)(2,1)} %collective-permute-done.25.refs_1_, ...), custom_call_target="tpu_custom_call" | custom-call | flops 1000000 | bytes 4128768 | tf_op jit(solution)/shard_map/core_sum/pallas_call | solution.py:847
  253.3 2.9 reduce-scatter.9.cloned.1.call-done
  256.2 1.0 copy-done
  257.2 3.7 %pair_sum.1 = bf16[4,4,96,384]{3,2,1,0:T(8,128)(2,1)} custom-call(bf16[4,4,96,384]{3,2,1,0:T(8,128)(2,1)} %get-tuple-element.152.mine_ref, bf16[4,4,96,384]{3,2,1,0:T(8,128)(2,1)} %copy-done, bf16[4,112,384]{2,1,0:T(8,128)(2,1)} %get-tuple-element.150.refs_11_.refs_0_, bf16[96,768]{1,0:T(8,128)(2,1)} %bitcast.44), custom_call_target="tpu_custom_call" | custom-call | flops 1000000 | bytes 3538944 | tf_op jit(solution)/shard_map/pair_sum/pallas_call | solution.py:865
  260.9 1.5 collective-permute-start.28
  262.4 1.5 collective-permute-start.32
  264.5 11.1 %input_gradient.1.refs_4_ = bf16[1024,768]{1,0:T(8,128)(2,1)} custom-call(s32[3]{0:T(128)} %pad_add_fusion.place_ref, f32[6]{0:T(128)} %scale_ref.9, bf16[304,768]{1,0:T(8,128)(2,1)} %get-tuple-element.106.refs_0_, bf16[304,768]{1,0:T(8,128)(2,1)} %copy-done.6, bf16[304,768]{1,0:T(8,128)(2,1)} %collective-permute-done.4.refs_2_, ...), custom_call_target="tpu_custom_call" | custom-call | flops 8999999488 | bytes 12976128 | tf_op jit(solution)/shard_map/input_gradient/pallas_call | solution.py:774
  275.6 3.8 %collective-permute-done.32.refs_2_ = bf16[4,112,384]{2,1,0:T(8,128)(2,1)S(1)} collective-permute-done((bf16[4,112,384]{2,1,0:T(8,128)(2,1)}, bf16[4,112,384]{2,1,0:T(8,128)(2,1)S(1)}, u32[]{:S(2)}, u32[]{:S(2)}) %collective-permute-start.32) | collective-permute-done | bytes 344096 | tf_op jit(solution)/shard_map/ppermute | solution.py:789
  279.4 0.7 copy-done.8
  280.1 0.7 copy-done.9
  280.8 2.1 plane_sum.3
  282.9 1.7 collective-permute-start.34
  285.3 2.0 collective-permute-start.36
  287.3 3.4 %reduce-scatter.11.cloned.1.call-done = bf16[1,4,96,384]{3,2,1,0:T(8,128)(2,1)} async-done(((bf16[4,4,96,384]{3,2,1,0:T(8,128)(2,1)}), bf16[1,4,96,384]{3,2,1,0:T(8,128)(2,1)}) %reduce-scatter.11.cloned.1.call-update) | async-done | bytes 294928 | tf_op jit(solution)/shard_map/reduce_scatter | solution.py:1077
  290.7 1.7 slice_bitcast_fusion
  292.4 4.0 %collective-permute-start.31 = (bf16[96,384]{1,0:T(8,128)(2,1)S(1)}, bf16[96,384]{1,0:T(8,128)(2,1)S(1)}, u32[]{:S(2)}, u32[]{:S(2)}) collective-permute-start(bf16[96,384]{1,0:T(8,128)(2,1)S(1)} %get-tuple-element.183), channel_id=1, source_target_pairs={{0,24},{4,28},{8,16},{12,20},{16,8},{20,12},{24,0},{28,4},{1,25},{... | collective-permute-start | bytes 221192 | tf_op jit(solution)/shard_map/ppermute | solution.py:789
  297.0 1.8 collective-permute-done.31.refs_3_
  298.8 1.9 collective-permute-done.30.refs_2_
  301.5 2.2 own_sums.1
  303.7 1.4 collective-permute-done.37
  305.8 0.7 collective-permute-start.40
  306.5 1.4 collective-permute-start.39
  307.9 1.3 collective-permute-start.38
  309.4 0.7 collective-permute-done.39
  310.1 2.3 collective-permute-done.38
  312.4 2.5 collective-permute-start.42
  314.9 1.9 collective-permute-start.41
  317.0 3.3 %collective-permute-done.41 = f32[8,128]{1,0:T(8,128)S(1)} collective-permute-done((f32[8,128]{1,0:T(8,128)S(1)}, f32[8,128]{1,0:T(8,128)S(1)}, u32[]{:S(2)}, u32[]{:S(2)}) %collective-permute-start.41) | collective-permute-done | bytes 4128 | tf_op jit(solution)/shard_map/ppermute | solution.py:789
  320.9 4.6 %state_update.1 = (f32[96,768]{1,0:T(8,128)}, f32[96,768]{1,0:T(8,128)}, f32[96,768]{1,0:T(8,128)}, f32[96,768]{1,0:T(8,128)}, f32[96,768]{1,0:T(8,128)}, /*inde...) custom-call(f32[8,128]{1,0:T(8,128)} %add_add_fusion.square_ref, ...), custom_call_target="tpu_custom_call" | custom-call | flops 10000000 | bytes 8000000 | tf_op jit(solution)/shard_map/state_update/pallas_call | solution.py:985
  (131 shorter events, 15.9 us)
Async XLA Ops:
  7.2 47.8 %all-gather.5.cloned.1.call-start = ((), (), s32[]{:S(2)}) async-start(), calls=%async_computation.8 | async-start | bytes 1327104 | tf_op jit(solution)/shard_map/all_gather | solution.py:1020
  7.9 112.8 %all-gather.7.cloned.1.call-start = ((), (), s32[]{:S(2)}) async-start(), calls=%async_computation.9 | async-start | bytes 2949120 | tf_op jit(solution)/shard_map/all_gather | solution.py:1023
  9.6 9.4 %copy-start.3 = (bf16[112,768]{1,0:T(8,128)(2,1)}, bf16[112,768]{1,0:T(8,128)(2,1)S(1)}, u32[]{:S(2)}) copy-start(bf16[112,768]{1,0:T(8,128)(2,1)S(1)} %fusion.1.refs_0_) | copy-start | bytes 516100
  9.6 10.4 %collective-permute-start.2 = (bf16[112,768]{1,0:T(8,128)(2,1)S(1)}, bf16[112,768]{1,0:T(8,128)(2,1)S(1)}, u32[]{:S(2)}, u32[]{:S(2)}) collective-permute-start(bf16[112,768]{1,0:T(8,128)(2,1)S(1)} %fusion.1.refs_0_), channel_id=1, source_target_pairs={{0,3},{1,2},{2,1},{3,0},{4,7},{5,6},{6,5},{7,4},{8,11},{9,10},{10,... | collective-permute-start | bytes 516104 | tf_op jit(solution)/shard_map/ppermute | solution.py:789
  14.7 14.6 %collective-permute-start.1 = (bf16[112,768]{1,0:T(8,128)(2,1)S(1)}, bf16[112,768]{1,0:T(8,128)(2,1)S(1)}, u32[]{:S(2)}, u32[]{:S(2)}) collective-permute-start(bf16[112,768]{1,0:T(8,128)(2,1)S(1)} %fusion.1.refs_0_), channel_id=1, source_target_pairs={{0,2},{1,3},{2,0},{3,1},{4,6},{5,7},{6,4},{7,5},{8,10},{9,11},{10,... | collective-permute-start | bytes 516104 | tf_op jit(solution)/shard_map/ppermute | solution.py:789
  14.7 14.6 %collective-permute-start = (bf16[112,768]{1,0:T(8,128)(2,1)S(1)}, bf16[112,768]{1,0:T(8,128)(2,1)S(1)}, u32[]{:S(2)}, u32[]{:S(2)}) collective-permute-start(bf16[112,768]{1,0:T(8,128)(2,1)S(1)} %fusion.1.refs_0_), channel_id=1, source_target_pairs={{0,1},{1,0},{2,3},{3,2},{4,5},{5,4},{6,7},{7,6},{8,9},{9,8},{10,11... | collective-permute-start | bytes 516104 | tf_op jit(solution)/shard_map/ppermute | solution.py:789
  19.0 17.2 %copy-start.13 = (bf16[96,768]{1,0:T(8,128)(2,1)S(1)}, bf16[96,768]{1,0:T(8,128)(2,1)}, u32[]{:S(2)}) copy-start(bf16[96,768]{1,0:T(8,128)(2,1)} %refs_0_.1) | copy-start | bytes 442372
  20.0 9.3 %copy-start.10 = (bf16[112,768]{1,0:T(8,128)(2,1)}, bf16[112,768]{1,0:T(8,128)(2,1)S(1)}, u32[]{:S(2)}) copy-start(bf16[112,768]{1,0:T(8,128)(2,1)S(1)} %collective-permute-done.2.refs_3_) | copy-start | bytes 516100
  32.7 24.6 %copy-start.26 = (bf16[304,768]{1,0:T(8,128)(2,1)S(1)}, bf16[304,768]{1,0:T(8,128)(2,1)}, u32[]{:S(2)}) copy-start(bf16[304,768]{1,0:T(8,128)(2,1)} %get-tuple-element.106.refs_0_) | copy-start | bytes 1400836
  32.7 19.2 %collective-permute-start.3 = (bf16[304,768]{1,0:T(8,128)(2,1)}, bf16[304,768]{1,0:T(8,128)(2,1)S(1)}, u32[]{:S(2)}, u32[]{:S(2)}) collective-permute-start(bf16[304,768]{1,0:T(8,128)(2,1)} %get-tuple-element.106.refs_0_), channel_id=1, source_target_pairs={{0,8},{4,12},{8,0},{12,4},{16,24},{20,28},{24,16},{28,20},{1,9},{5... | collective-permute-start | bytes 1400840 | tf_op jit(solution)/shard_map/ppermute | solution.py:789
  34.2 22.7 %collective-permute-start.5 = (bf16[304,768]{1,0:T(8,128)(2,1)}, bf16[304,768]{1,0:T(8,128)(2,1)}, u32[]{:S(2)}, u32[]{:S(2)}) collective-permute-start(bf16[304,768]{1,0:T(8,128)(2,1)} %get-tuple-element.106.refs_0_), channel_id=1, source_target_pairs={{0,24},{4,28},{8,16},{12,20},{16,8},{20,12},{24,0},{28,4},{1,25},{... | collective-permute-start | bytes 1400840 | tf_op jit(solution)/shard_map/ppermute | solution.py:789
  35.7 21.6 %collective-permute-start.4 = (bf16[304,768]{1,0:T(8,128)(2,1)}, bf16[304,768]{1,0:T(8,128)(2,1)}, u32[]{:S(2)}, u32[]{:S(2)}) collective-permute-start(bf16[304,768]{1,0:T(8,128)(2,1)} %get-tuple-element.106.refs_0_), channel_id=1, source_target_pairs={{0,16},{4,20},{8,24},{12,28},{16,0},{20,4},{24,8},{28,12},{1,17},{... | collective-permute-start | bytes 1400840 | tf_op jit(solution)/shard_map/ppermute | solution.py:789
  36.2 7.6 %collective-permute-start.8 = (bf16[96,768]{1,0:T(8,128)(2,1)S(1)}, bf16[96,768]{1,0:T(8,128)(2,1)S(1)}, u32[]{:S(2)}, u32[]{:S(2)}) collective-permute-start(bf16[96,768]{1,0:T(8,128)(2,1)S(1)} %copy-done.13), channel_id=1, source_target_pairs={{0,3},{1,2},{2,1},{3,0},{4,7},{5,6},{6,5},{7,4},{8,11},{9,10},{10,... | collective-permute-start | bytes 442376 | tf_op jit(solution)/shard_map/ppermute | solution.py:789
  38.7 11.2 %collective-permute-start.7 = (bf16[96,768]{1,0:T(8,128)(2,1)S(1)}, bf16[96,768]{1,0:T(8,128)(2,1)S(1)}, u32[]{:S(2)}, u32[]{:S(2)}) collective-permute-start(bf16[96,768]{1,0:T(8,128)(2,1)S(1)} %copy-done.13), channel_id=1, source_target_pairs={{0,2},{1,3},{2,0},{3,1},{4,6},{5,7},{6,4},{7,5},{8,10},{9,11},{10,... | collective-permute-start | bytes 442376 | tf_op jit(solution)/shard_map/ppermute | solution.py:789
  43.9 8.1 %copy-start.14 = (bf16[96,768]{1,0:T(8,128)(2,1)}, bf16[96,768]{1,0:T(8,128)(2,1)S(1)}, u32[]{:S(2)}) copy-start(bf16[96,768]{1,0:T(8,128)(2,1)S(1)} %collective-permute-done.8.refs_3_) | copy-start | bytes 442372
  43.9 8.0 %collective-permute-start.6 = (bf16[96,768]{1,0:T(8,128)(2,1)S(1)}, bf16[96,768]{1,0:T(8,128)(2,1)S(1)}, u32[]{:S(2)}, u32[]{:S(2)}) collective-permute-start(bf16[96,768]{1,0:T(8,128)(2,1)S(1)} %copy-done.13), channel_id=1, source_target_pairs={{0,1},{1,0},{2,3},{3,2},{4,5},{5,4},{6,7},{7,6},{8,9},{9,8},{10,11... | collective-permute-start | bytes 442376 | tf_op jit(solution)/shard_map/ppermute | solution.py:789
  54.9 4.8 %copy-start.2 = (bf16[480,768]{1,0:T(8,128)(2,1)S(1)}, bf16[480,768]{1,0:T(8,128)(2,1)}, u32[]{:S(2)}) copy-start(bf16[480,768]{1,0:T(8,128)(2,1)} %weight_order.1.refs_8_.refs_0_.refs_2_) | copy-start | bytes 2211844
  57.3 2.5 collective-permute-start.10
  57.3 4.3 %collective-permute-start.11 = (bf16[304,768]{1,0:T(8,128)(2,1)}, bf16[304,768]{1,0:T(8,128)(2,1)S(1)}, u32[]{:S(2)}, u32[]{:S(2)}) collective-permute-start(bf16[304,768]{1,0:T(8,128)(2,1)} %copy-done.6), channel_id=1, source_target_pairs={{0,4},{4,0},{8,12},{12,8},{16,20},{20,16},{24,28},{28,24},{1,5},{5... | collective-permute-start | bytes 1400840 | tf_op jit(solution)/shard_map/ppermute | solution.py:789
  57.8 4.9 %collective-permute-start.12 = (bf16[304,768]{1,0:T(8,128)(2,1)}, bf16[304,768]{1,0:T(8,128)(2,1)S(1)}, u32[]{:S(2)}, u32[]{:S(2)}) collective-permute-start(bf16[304,768]{1,0:T(8,128)(2,1)} %collective-permute-done.4.refs_2_), channel_id=1, source_target_pairs={{0,4},{4,0},{8,12},{12,8},{16,20},{20,16},{24,28},{28,24},{1,5},{5... | collective-permute-start | bytes 1400840 | tf_op jit(solution)/shard_map/ppermute | solution.py:789
  57.8 5.7 %collective-permute-start.13 = (bf16[304,768]{1,0:T(8,128)(2,1)}, bf16[304,768]{1,0:T(8,128)(2,1)}, u32[]{:S(2)}, u32[]{:S(2)}) collective-permute-start(bf16[304,768]{1,0:T(8,128)(2,1)} %collective-permute-done.5.refs_3_), channel_id=1, source_target_pairs={{0,4},{4,0},{8,12},{12,8},{16,20},{20,16},{24,28},{28,24},{1,5},{5... | collective-permute-start | bytes 1400840 | tf_op jit(solution)/shard_map/ppermute | solution.py:789
  59.0 36.7 %collective-permute-start.16 = (bf16[480,768]{1,0:T(8,128)(2,1)}, bf16[480,768]{1,0:T(8,128)(2,1)S(1)}, u32[]{:S(2)}, u32[]{:S(2)}) collective-permute-start(bf16[480,768]{1,0:T(8,128)(2,1)} %weight_order.1.refs_8_.refs_0_.refs_2_), channel_id=1, source_target_pairs={{0,4},{4,0},{8,12},{12,8},{16,20},{20,16},{24,28},{28,24},{1,5},{5... | collective-permute-start | bytes 2211848 | tf_op jit(solution)/shard_map/ppermute | solution.py:789
  59.1 146.4 %reduce-scatter.5.cloned.1.call-start = ((), (), s32[]{:S(2)}) async-start(), calls=%async_computation.4 | async-start | bytes 5308416 | tf_op jit(solution)/shard_map/reduce_scatter | solution.py:1061
  59.8 3.6 %copy-start.27 = (bf16[304,768]{1,0:T(8,128)(2,1)}, bf16[304,768]{1,0:T(8,128)(2,1)S(1)}, u32[]{:S(2)}) copy-start(bf16[304,768]{1,0:T(8,128)(2,1)S(1)} %collective-permute-done.10.refs_4_) | copy-start | bytes 1400836
  59.8 33.9 %collective-permute-start.15 = (bf16[480,768]{1,0:T(8,128)(2,1)S(1)}, bf16[480,768]{1,0:T(8,128)(2,1)}, u32[]{:S(2)}, u32[]{:S(2)}) collective-permute-start(bf16[480,768]{1,0:T(8,128)(2,1)S(1)} %copy-done.2), channel_id=1, source_target_pairs={{0,24},{4,28},{8,16},{12,20},{16,8},{20,12},{24,0},{28,4},{1,25},{... | collective-permute-start | bytes 2211848 | tf_op jit(solution)/shard_map/ppermute | solution.py:789
  61.6 33.5 %collective-permute-start.14 = (bf16[480,768]{1,0:T(8,128)(2,1)S(1)}, bf16[480,768]{1,0:T(8,128)(2,1)}, u32[]{:S(2)}, u32[]{:S(2)}) collective-permute-start(bf16[480,768]{1,0:T(8,128)(2,1)S(1)} %copy-done.2), channel_id=1, source_target_pairs={{0,16},{4,20},{8,24},{12,28},{16,0},{20,4},{24,8},{28,12},{1,17},{... | collective-permute-start | bytes 2211848 | tf_op jit(solution)/shard_map/ppermute | solution.py:789
  62.7 32.4 %collective-permute-start.9 = (bf16[480,768]{1,0:T(8,128)(2,1)S(1)}, bf16[480,768]{1,0:T(8,128)(2,1)}, u32[]{:S(2)}, u32[]{:S(2)}) collective-permute-start(bf16[480,768]{1,0:T(8,128)(2,1)S(1)} %copy-done.2), channel_id=1, source_target_pairs={{0,8},{4,12},{8,0},{12,4},{16,24},{20,28},{24,16},{28,20},{1,9},{5... | collective-permute-start | bytes 2211848 | tf_op jit(solution)/shard_map/ppermute | solution.py:789
  95.1 3.1 collective-permute-start.17
  95.2 3.6 %collective-permute-start.18 = (bf16[480,768]{1,0:T(8,128)(2,1)}, bf16[480,768]{1,0:T(8,128)(2,1)}, u32[]{:S(2)}, u32[]{:S(2)}) collective-permute-start(bf16[480,768]{1,0:T(8,128)(2,1)} %collective-permute-done.14.refs_2_.refs_4_), channel_id=1, source_target_pairs={{0,4},{4,0},{8,12},{12,8},{16,20},{20,16},{24,28},{28,24},{1,5},{5... | collective-permute-start | bytes 2211848 | tf_op jit(solution)/shard_map/ppermute | solution.py:789
  95.7 4.2 %collective-permute-start.19 = (bf16[480,768]{1,0:T(8,128)(2,1)}, bf16[480,768]{1,0:T(8,128)(2,1)}, u32[]{:S(2)}, u32[]{:S(2)}) collective-permute-start(bf16[480,768]{1,0:T(8,128)(2,1)} %collective-permute-done.15.refs_3_.refs_5_), channel_id=1, source_target_pairs={{0,4},{4,0},{8,12},{12,8},{16,20},{20,16},{24,28},{28,24},{1,5},{5... | collective-permute-start | bytes 2211848 | tf_op jit(solution)/shard_map/ppermute | solution.py:789
  95.7 4.1 %copy-start.24 = (bf16[480,768]{1,0:T(8,128)(2,1)}, bf16[480,768]{1,0:T(8,128)(2,1)S(1)}, u32[]{:S(2)}) copy-start(bf16[480,768]{1,0:T(8,128)(2,1)S(1)} %collective-permute-done.16.refs_4_.refs_6_) | copy-start | bytes 2211844
  120.7 4.9 %collective-permute-start.20 = (bf16[4,4,192,384]{3,2,1,0:T(8,128)(2,1)}, bf16[4,4,192,384]{3,2,1,0:T(8,128)(2,1)}, u32[]{:S(2)}, u32[]{:S(2)}) collective-permute-start(bf16[4,4,192,384]{3,2,1,0:T(8,128)(2,1)} %bitcast.60), channel_id=1, source_target_pairs={{0,4},{4,0},{8,12},{12,8},{16,20},{20,16},{24,28},{28,24},{1,5},{5... | collective-permute-start | bytes 7077896 | tf_op jit(solution)/shard_map/ppermute | solution.py:789
  147.3 84.5 %reduce-scatter.7.cloned.1.call-start = ((), (), s32[]{:S(2)}) async-start(), calls=%async_computation.5 | async-start | bytes 737280 | tf_op jit(solution)/shard_map/reduce_scatter | solution.py:1068
  147.3 31.3 %copy-start.23 = (f32[8,768]{1,0:T(8,128)S(1)}, f32[8,768]{1,0:T(8,128)}, u32[]{:S(2)}) copy-start(f32[8,768]{1,0:T(8,128)} %get-tuple-element.142) | copy-start | bytes 73732
  178.5 19.1 %collective-permute-start.21 = (bf16[4,4,96,768]{3,2,1,0:T(8,128)(2,1)}, bf16[4,4,96,768]{3,2,1,0:T(8,128)(2,1)}, u32[]{:S(2)}, u32[]{:S(2)}) collective-permute-start(bf16[4,4,96,768]{3,2,1,0:T(8,128)(2,1)} %get-tuple-element.132.refs_0_), channel_id=1, source_target_pairs={{0,4},{4,0},{8,12},{12,8},{16,20},{20,16},{24,28},{28,24},{1,5},{5... | collective-permute-start | bytes 7077896 | tf_op jit(solution)/shard_map/ppermute | solution.py:789
  202.0 29.5 %collective-permute-start.22 = (bf16[4,96,768]{2,1,0:T(8,128)(2,1)}, bf16[4,96,768]{2,1,0:T(8,128)(2,1)S(1)}, u32[]{:S(2)}, u32[]{:S(2)}) collective-permute-start(bf16[4,96,768]{2,1,0:T(8,128)(2,1)} %get-tuple-element.136), channel_id=1, source_target_pairs={{0,8},{4,12},{8,0},{12,4},{16,24},{20,28},{24,16},{28,20},{1,9},{5... | collective-permute-start | bytes 1769480 | tf_op jit(solution)/shard_map/ppermute | solution.py:789
  202.0 29.7 %collective-permute-start.23 = (bf16[4,96,768]{2,1,0:T(8,128)(2,1)}, bf16[4,96,768]{2,1,0:T(8,128)(2,1)S(1)}, u32[]{:S(2)}, u32[]{:S(2)}) collective-permute-start(bf16[4,96,768]{2,1,0:T(8,128)(2,1)} %get-tuple-element.137), channel_id=1, source_target_pairs={{0,16},{4,20},{8,24},{12,28},{16,0},{20,4},{24,8},{28,12},{1,17},{... | collective-permute-start | bytes 1769480 | tf_op jit(solution)/shard_map/ppermute | solution.py:789
  204.7 27.0 %collective-permute-start.24 = (bf16[4,96,768]{2,1,0:T(8,128)(2,1)}, bf16[4,96,768]{2,1,0:T(8,128)(2,1)}, u32[]{:S(2)}, u32[]{:S(2)}) collective-permute-start(bf16[4,96,768]{2,1,0:T(8,128)(2,1)} %get-tuple-element.138), channel_id=1, source_target_pairs={{0,24},{4,28},{8,16},{12,20},{16,8},{20,12},{24,0},{28,4},{1,25},{... | collective-permute-start | bytes 1769480 | tf_op jit(solution)/shard_map/ppermute | solution.py:789
  205.5 50.7 %reduce-scatter.9.cloned.1.call-start = ((), (), s32[]{:S(2)}) async-start(), calls=%async_computation.6 | async-start | bytes 737280 | tf_op jit(solution)/shard_map/reduce_scatter | solution.py:1070
  231.4 16.0 %collective-permute-start.26 = (bf16[4,4,96,256]{3,2,1,0:T(8,128)(2,1)}, bf16[4,4,96,256]{3,2,1,0:T(8,128)(2,1)S(1)}, u32[]{:S(2)}, u32[]{:S(2)}) collective-permute-start(bf16[4,4,96,256]{3,2,1,0:T(8,128)(2,1)} %get-tuple-element.149), channel_id=1, source_target_pairs={{0,4},{4,0},{8,12},{12,8},{16,20},{20,16},{24,28},{28,24},{1,5},{5... | collective-permute-start | bytes 2359304 | tf_op jit(solution)/shard_map/ppermute | solution.py:789
  235.3 55.5 %reduce-scatter.11.cloned.1.call-start = ((), (), s32[]{:S(2)}) async-start(), calls=%async_computation.7 | async-start | bytes 1474560 | tf_op jit(solution)/shard_map/reduce_scatter | solution.py:1077
  235.3 20.9 %collective-permute-start.27 = (bf16[4,4,96,384]{3,2,1,0:T(8,128)(2,1)}, bf16[4,4,96,384]{3,2,1,0:T(8,128)(2,1)S(1)}, u32[]{:S(2)}, u32[]{:S(2)}) collective-permute-start(bf16[4,4,96,384]{3,2,1,0:T(8,128)(2,1)} %get-tuple-element.154), channel_id=1, source_target_pairs={{0,4},{4,0},{8,12},{12,8},{16,20},{20,16},{24,28},{28,24},{1,5},{5... | collective-permute-start | bytes 3538952 | tf_op jit(solution)/shard_map/ppermute | solution.py:789
  247.3 2.2 collective-permute-start.25
  247.4 2.1 copy-start.1
  260.9 14.6 %collective-permute-start.28 = (bf16[4,112,384]{2,1,0:T(8,128)(2,1)}, bf16[4,112,384]{2,1,0:T(8,128)(2,1)S(1)}, u32[]{:S(2)}, u32[]{:S(2)}) collective-permute-start(bf16[4,112,384]{2,1,0:T(8,128)(2,1)} %get-tuple-element.155), channel_id=1, source_target_pairs={{0,8},{4,12},{8,0},{12,4},{16,24},{20,28},{24,16},{28,20},{1,9},{5... | collective-permute-start | bytes 1032200 | tf_op jit(solution)/shard_map/ppermute | solution.py:789
  262.4 16.9 %collective-permute-start.32 = (bf16[4,112,384]{2,1,0:T(8,128)(2,1)}, bf16[4,112,384]{2,1,0:T(8,128)(2,1)S(1)}, u32[]{:S(2)}, u32[]{:S(2)}) collective-permute-start(bf16[4,112,384]{2,1,0:T(8,128)(2,1)} %get-tuple-element.157), channel_id=1, source_target_pairs={{0,16},{4,20},{8,24},{12,28},{16,0},{20,4},{24,8},{28,12},{1,17},{... | collective-permute-start | bytes 1032200 | tf_op jit(solution)/shard_map/ppermute | solution.py:789
  263.9 15.5 %collective-permute-start.33 = (bf16[4,112,384]{2,1,0:T(8,128)(2,1)}, bf16[4,112,384]{2,1,0:T(8,128)(2,1)S(1)}, u32[]{:S(2)}, u32[]{:S(2)}) collective-permute-start(bf16[4,112,384]{2,1,0:T(8,128)(2,1)} %get-tuple-element.158), channel_id=1, source_target_pairs={{0,24},{4,28},{8,16},{12,20},{16,8},{20,12},{24,0},{28,4},{1,25},{... | collective-permute-start | bytes 1032200 | tf_op jit(solution)/shard_map/ppermute | solution.py:789
  275.6 3.8 %copy-start.7 = (bf16[4,112,384]{2,1,0:T(8,128)(2,1)}, bf16[4,112,384]{2,1,0:T(8,128)(2,1)S(1)}, u32[]{:S(2)}) copy-start(bf16[4,112,384]{2,1,0:T(8,128)(2,1)S(1)} %collective-permute-done.28.refs_1_) | copy-start | bytes 1032196
  282.9 13.5 %collective-permute-start.34 = (bf16[112,384]{1,0:T(8,128)(2,1)}, bf16[112,384]{1,0:T(8,128)(2,1)S(1)}, u32[]{:S(2)}, u32[]{:S(2)}) collective-permute-start(bf16[112,384]{1,0:T(8,128)(2,1)} %get-tuple-element.160), channel_id=1, source_target_pairs={{0,1},{1,0},{2,3},{3,2},{4,5},{5,4},{6,7},{7,6},{8,9},{9,8},{10,11... | collective-permute-start | bytes 258056 | tf_op jit(solution)/shard_map/ppermute | solution.py:789
  284.6 12.3 %collective-permute-start.35 = (bf16[112,384]{1,0:T(8,128)(2,1)}, bf16[112,384]{1,0:T(8,128)(2,1)S(1)}, u32[]{:S(2)}, u32[]{:S(2)}) collective-permute-start(bf16[112,384]{1,0:T(8,128)(2,1)} %get-tuple-element.161), channel_id=1, source_target_pairs={{0,2},{1,3},{2,0},{3,1},{4,6},{5,7},{6,4},{7,5},{8,10},{9,11},{10,... | collective-permute-start | bytes 258056 | tf_op jit(solution)/shard_map/ppermute | solution.py:789
  285.3 11.7 %collective-permute-start.36 = (bf16[112,384]{1,0:T(8,128)(2,1)}, bf16[112,384]{1,0:T(8,128)(2,1)S(1)}, u32[]{:S(2)}, u32[]{:S(2)}) collective-permute-start(bf16[112,384]{1,0:T(8,128)(2,1)} %get-tuple-element.162), channel_id=1, source_target_pairs={{0,3},{1,2},{2,1},{3,0},{4,7},{5,6},{6,5},{7,4},{8,11},{9,10},{10,... | collective-permute-start | bytes 258056 | tf_op jit(solution)/shard_map/ppermute | solution.py:789
  292.4 6.4 %collective-permute-start.31 = (bf16[96,384]{1,0:T(8,128)(2,1)S(1)}, bf16[96,384]{1,0:T(8,128)(2,1)S(1)}, u32[]{:S(2)}, u32[]{:S(2)}) collective-permute-start(bf16[96,384]{1,0:T(8,128)(2,1)S(1)} %get-tuple-element.183), channel_id=1, source_target_pairs={{0,24},{4,28},{8,16},{12,20},{16,8},{20,12},{24,0},{28,4},{1,25},{... | collective-permute-start | bytes 221192 | tf_op jit(solution)/shard_map/ppermute | solution.py:789
  296.4 4.4 %collective-permute-start.30 = (bf16[96,384]{1,0:T(8,128)(2,1)S(1)}, bf16[96,384]{1,0:T(8,128)(2,1)S(1)}, u32[]{:S(2)}, u32[]{:S(2)}) collective-permute-start(bf16[96,384]{1,0:T(8,128)(2,1)S(1)} %get-tuple-element.184), channel_id=1, source_target_pairs={{0,16},{4,20},{8,24},{12,28},{16,0},{20,4},{24,8},{28,12},{1,17},{... | collective-permute-start | bytes 221192 | tf_op jit(solution)/shard_map/ppermute | solution.py:789
  296.4 4.4 %copy-start.17 = (bf16[112,384]{1,0:T(8,128)(2,1)}, bf16[112,384]{1,0:T(8,128)(2,1)S(1)}, u32[]{:S(2)}) copy-start(bf16[112,384]{1,0:T(8,128)(2,1)S(1)} %collective-permute-done.34.refs_5_) | copy-start | bytes 258052
  296.4 4.4 %collective-permute-start.29 = (bf16[96,384]{1,0:T(8,128)(2,1)S(1)}, bf16[96,384]{1,0:T(8,128)(2,1)S(1)}, u32[]{:S(2)}, u32[]{:S(2)}) collective-permute-start(bf16[96,384]{1,0:T(8,128)(2,1)S(1)} %get-tuple-element.185), channel_id=1, source_target_pairs={{0,8},{4,12},{8,0},{12,4},{16,24},{20,28},{24,16},{28,20},{1,9},{5... | collective-permute-start | bytes 221192 | tf_op jit(solution)/shard_map/ppermute | solution.py:789
  297.0 3.9 %copy-start.18 = (bf16[112,384]{1,0:T(8,128)(2,1)}, bf16[112,384]{1,0:T(8,128)(2,1)S(1)}, u32[]{:S(2)}) copy-start(bf16[112,384]{1,0:T(8,128)(2,1)S(1)} %collective-permute-done.35.refs_6_) | copy-start | bytes 258052
  297.0 3.9 %copy-start.19 = (bf16[112,384]{1,0:T(8,128)(2,1)}, bf16[112,384]{1,0:T(8,128)(2,1)S(1)}, u32[]{:S(2)}) copy-start(bf16[112,384]{1,0:T(8,128)(2,1)S(1)} %collective-permute-done.36.refs_7_) | copy-start | bytes 258052
  303.7 1.4 collective-permute-start.37
  305.8 3.6 %collective-permute-start.40 = (f32[8,128]{1,0:T(8,128)S(1)}, f32[8,128]{1,0:T(8,128)S(1)}, u32[]{:S(2)}, u32[]{:S(2)}) collective-permute-start(f32[8,128]{1,0:T(8,128)S(1)} %add.36), channel_id=1, source_target_pairs={{0,8},{4,12},{8,0},{12,4},{16,24},{20,28},{24,16},{28,20},{1,9},{5... | collective-permute-start | bytes 12296 | tf_op jit(solution)/shard_map/ppermute | solution.py:789
  306.5 3.6 %collective-permute-start.39 = (f32[8,128]{1,0:T(8,128)S(1)}, f32[8,128]{1,0:T(8,128)S(1)}, u32[]{:S(2)}, u32[]{:S(2)}) collective-permute-start(f32[8,128]{1,0:T(8,128)S(1)} %add.36), channel_id=1, source_target_pairs={{0,16},{4,20},{8,24},{12,28},{16,0},{20,4},{24,8},{28,12},{1,17},{... | collective-permute-start | bytes 12296 | tf_op jit(solution)/shard_map/ppermute | solution.py:789
  307.9 4.5 %collective-permute-start.38 = (f32[8,128]{1,0:T(8,128)S(1)}, f32[8,128]{1,0:T(8,128)S(1)}, u32[]{:S(2)}, u32[]{:S(2)}) collective-permute-start(f32[8,128]{1,0:T(8,128)S(1)} %add.36), channel_id=1, source_target_pairs={{0,24},{4,28},{8,16},{12,20},{16,8},{20,12},{24,0},{28,4},{1,25},{... | collective-permute-start | bytes 12296 | tf_op jit(solution)/shard_map/ppermute | solution.py:789
  312.4 4.4 %collective-permute-start.43 = (f32[8,128]{1,0:T(8,128)S(1)}, f32[8,128]{1,0:T(8,128)S(1)}, u32[]{:S(2)}, u32[]{:S(2)}) collective-permute-start(f32[8,128]{1,0:T(8,128)S(1)} %add_add_fusion.1), channel_id=1, source_target_pairs={{0,1},{1,0},{2,3},{3,2},{4,5},{5,4},{6,7},{7,6},{8,9},{9,8},{10,11... | collective-permute-start | bytes 12296 | tf_op jit(solution)/shard_map/ppermute | solution.py:789
  312.4 4.6 %collective-permute-start.42 = (f32[8,128]{1,0:T(8,128)S(1)}, f32[8,128]{1,0:T(8,128)S(1)}, u32[]{:S(2)}, u32[]{:S(2)}) collective-permute-start(f32[8,128]{1,0:T(8,128)S(1)} %add_add_fusion.1), channel_id=1, source_target_pairs={{0,2},{1,3},{2,0},{3,1},{4,6},{5,7},{6,4},{7,5},{8,10},{9,11},{10,... | collective-permute-start | bytes 12296 | tf_op jit(solution)/shard_map/ppermute | solution.py:789
  314.9 5.4 %collective-permute-start.41 = (f32[8,128]{1,0:T(8,128)S(1)}, f32[8,128]{1,0:T(8,128)S(1)}, u32[]{:S(2)}, u32[]{:S(2)}) collective-permute-start(f32[8,128]{1,0:T(8,128)S(1)} %add_add_fusion.1), channel_id=1, source_target_pairs={{0,3},{1,2},{2,1},{3,0},{4,7},{5,6},{6,5},{7,4},{8,11},{9,10},{10,... | collective-permute-start | bytes 12296 | tf_op jit(solution)/shard_map/ppermute | solution.py:789
  (16 other events, 16.3 us)
Sparse Core Ops, SparseCore 0:
  9.9 27.0 all-gather.4
  59.2 49.9 all-gather.6
  147.4 53.3 reduce-scatter.4
  205.6 20.5 reduce-scatter.6
  235.4 20.7 reduce-scatter.8
  261.1 29.6 reduce-scatter.10
where the time goes:
time: 336 us; the launch traced here: 333 us
  Pallas kernels  201 us (60%)
  waiting for transfers between devices  54.7 us (16%)
  starting transfers between devices  47.3 us (14%)
  between operations  15.6 us (5%)
  local copies, waits for them, and re-layouts  9.92 us (3%)
  other arithmetic  4.84 us (1%)
    pallas_call x3, Pallas kernels, attn_bwd(): pl.pallas_call(functools.partial(attn_bwd_kernel, block=512, cores=cores,...  54.8 us
    ppermute x44, waiting for transfers between devices, swap(): return lax.ppermute(value, axis, [(i, i ^ mask) for i in range(count)])  47.6 us
    ppermute x44, starting transfers between devices, swap(): return lax.ppermute(value, axis, [(i, i ^ mask) for i in range(count)])  46.9 us
    pallas_call x1, Pallas kernels, mid_bwd(): pl.pallas_call(functools.partial(mid_bwd_kernel, chunk=256, count=count,...  31.1 us
    pallas_call x1, Pallas kernels, attn_fwd(): pl.pallas_call(functools.partial(attn_fwd_kernel, block=512, count=count,...  27.1 us
    pallas_call x1, Pallas kernels, second_norm(): pl.pallas_call(functools.partial(second_norm_kernel, cores=len(downs), ti...  21.6 us
    pallas_call x1, Pallas kernels, mid_fwd(): pl.pallas_call(functools.partial(mid_fwd_kernel, chunk=256, count=count,...  20.9 us
    pallas_call x1, Pallas kernels, input_grad(): pl.pallas_call(functools.partial(input_grad_kernel, count=count, chunks=c...  11.1 us
  transfers between devices with their start and end apart: 50, of which 26 were waited for; matrix products, arithmetic and copies ran while one was open for 2% of the time, Pallas kernels for 51%

commit v1 on v0

--- a/solution.py
+++ b/solution.py
@@ -310,7 +310,7 @@
 ):
     refs = refs[deps:]
     if last:
-        before_a_ref, before_b_ref, vg_ref, b1g_ref, *refs = refs
+        before_a_ref, before_b_ref, vg_first_ref, vg_second_ref, b1g_ref, *refs = refs
     grads = refs[:cores]
     dqkv_ref, sum_ref, dk_acc, dv_acc, dq_acc, x_t, c_t, sems = refs[cores:]
     rows = q_ref.shape[0]
@@ -393,7 +393,8 @@
         def _():
             sum_ref[0:2, : before_a_ref.shape[1]] = before_a_ref[0:2, :]
             sum_ref[0:2, low + span_cols :] = before_b_ref[0:2, :]
-            sum_ref[2:8, :] = vg_ref[2:8, :]
+            sum_ref[2:5, :] = vg_first_ref[2:5, :]
+            sum_ref[5:8, :] = vg_second_ref[5:8, :]
             for row in range(b1g_ref.shape[1] // total_width):
                 sum_ref[8 + row : 9 + row, :] = b1g_ref[0:1, row * total_width : (row + 1) * total_width]
 
@@ -830,10 +831,10 @@
     for index, (depth, width) in enumerate(sizes):
         mine, got = refs[2 * index : 2 * index + 2]
         for spot, out in enumerate(outs):
-            total = mine[spot, 0].astype(f32) + got[spot, 0].astype(f32)
-            out[0, :depth, at : at + width] = total.astype(bf16)
+            out[:, :depth, at : at + width] = mine[spot] + got[spot]
             if depth < out.shape[1]:
-                out[0, depth:, at : at + width] = jnp.zeros((out.shape[1] - depth, width), bf16)
+                rest = (out.shape[0], out.shape[1] - depth, width)
+                out[:, depth:, at : at + width] = jnp.zeros(rest, bf16)
         at += width
 
 
@@ -842,13 +843,13 @@
     sizes = [mine.shape[2:] for mine, _ in pairs]
     rows, width = max(s[0] for s in sizes), sum(s[1] for s in sizes)
     specs = []
-    for mine, got in pairs:
-        specs += [pl.BlockSpec((spots, 1) + mine.shape[2:], lambda i: (0, i, 0, 0))] * 2
+    for depth, wide in sizes:
+        specs += [pl.BlockSpec((spots, 2, depth, wide), lambda i: (0, i, 0, 0))] * 2
     return pl.pallas_call(
         functools.partial(core_sum_kernel, sizes=sizes, deps=len(deps)),
-        grid=(slots,),
+        grid=(slots // 2,),
         in_specs=specs + [ANY] * len(deps),
-        out_specs=[pl.BlockSpec((1, rows, width), lambda i: (i, 0, 0))] * spots,
+        out_specs=[pl.BlockSpec((2, rows, width), lambda i: (i, 0, 0))] * spots,
         out_shape=[SDS((slots, rows, width), bf16)] * spots,
         compiler_params=params(),
         cost_estimate=cost(1e6, 6 * spots * slots * rows * width),
@@ -857,14 +858,14 @@
 
 
 def pair_sum_kernel(mine_ref, got_ref, *refs):
-    refs[-1][...] = (mine_ref[...].astype(f32) + got_ref[...].astype(f32)).astype(bf16)
+    refs[-1][...] = mine_ref[...] + got_ref[...]
 
 
 def pair_sum(mine, got, deps=()):
-    block = pl.BlockSpec((1,) + mine.shape[1:], lambda i: (i, 0, 0, 0))
+    block = pl.BlockSpec((2,) + mine.shape[1:], lambda i: (i, 0, 0, 0))
     return pl.pallas_call(
         pair_sum_kernel,
-        grid=mine.shape[:1],
+        grid=(mine.shape[0] // 2,),
         in_specs=[block, block] + [ANY] * len(deps),
         out_specs=block,
         out_shape=SDS(mine.shape, bf16),
@@ -1053,7 +1054,6 @@
     dh, dh_low, dc, vec_first, b1_grad, *up_parts = mid_bwd(
         place, quant_scales, ups, downs, n1, r1, y1, gelu_grad, dz, dz_low, vec, cores, spots, [grad_down]
     )
-    vec_grad = jnp.concatenate([vec_first[:5], vec_second[5:]])
     attn = functools.partial(
         attn_bwd, place, first_lengths, q, k, v, dc, c, lse, x_turned, c_turned, dh_low, cores=cores, spots=spots
     )
@@ -1069,10 +1069,10 @@
         (up_shards,) = plane_sum([up_plane], False, [d_q, own_down])
         own_up = lax.psum_scatter(up_shards, "shard", scatter_dimension=0)
         got_q = swap(after(parts_q[1], up_shards), "dp", 1)
-        *parts_r, d_r, sums = attn(first=3, pairs=1, deps=[up_shards], before=(sums_q, sums_p, vec_grad, b1_grad))
+        *parts_r, d_r, sums = attn(first=3, pairs=1, deps=[up_shards], before=(sums_q, sums_p, vec_first, vec_second, b1_grad))
         got_r = swap(parts_r[1], "dp", 1)
-        plane_pr = core_sum([(parts_r[0], got_r), (parts_p[0], got_p)], [d_r])
-        sum_q = pair_sum(parts_q[0], got_q, [plane_pr[0], own_up])
+        sum_q = pair_sum(parts_q[0], got_q, [d_r])
+        plane_pr = core_sum([(parts_r[0], got_r), (parts_p[0], got_p)], [sum_q, own_up])
         plane_pr = exchange(plane_pr, "dp", 2)
         spots_q = lax.psum_scatter(sum_q, "shard", scatter_dimension=0)
         spots_q = exchange(after(spots_q, plane_pr[1]), "dp", 2)
@@ -1081,7 +1081,7 @@
     else:
         parts_p, d_p, sums_p = attn(first=4, pairs=2, deps=[])
         parts_q, d_q, sums_q = attn(first=0, pairs=3, deps=[])
-        parts_r, d_r, sums = attn(first=3, pairs=1, deps=[], before=(sums_q, sums_p, vec_grad, b1_grad))
+        parts_r, d_r, sums = attn(first=3, pairs=1, deps=[], before=(sums_q, sums_p, vec_first, vec_second, b1_grad))
         attn_parts = [[parts_q], [parts_r], [parts_p]]
         input_gradient = input_grad(place, quant_scales, pieces, [d_q, d_r, d_p], dh, [])
 

time: 336 us -> 329 us (0.979)
  waiting for transfers between devices: 54.7 us -> 48.1 us
  Pallas kernels: 201 us -> 197 us
    reduce_scatter x1, waiting for transfers between devices: 3.42 us -> 0.01 us  [on_device(): spots_q = lax.psum_scatter(sum_q, 'shard', scatter_dimension=0)]
    unnamed x60 -> x64, local copies, waits for them, and re-layouts: 6.25 us -> 7.34 us
  transfers between devices with their start and end apart: 50 -> 50, of which waited for: 26 -> 25; matrix products, arithmetic and copies ran while one was open for 2% -> 2% of each run, Pallas kernels for 51% -> 51%
where the time goes in v1:
time: 329 us; the launch traced here: 326 us
  Pallas kernels  197 us (60%)
  starting transfers between devices  50.1 us (15%)
  waiting for transfers between devices  48.1 us (15%)
  between operations  15.6 us (5%)
  local copies, waits for them, and re-layouts  11 us (3%)
  other arithmetic  3.49 us (1%)
    pallas_call x3, Pallas kernels, attn_bwd(): pl.pallas_call(functools.partial(attn_bwd_kernel, block=512, cores=cores,...  55 us
    ppermute x44, starting transfers between devices, swap(): return lax.ppermute(value, axis, [(i, i ^ mask) for i in range(count)])  49.6 us
    ppermute x44, waiting for transfers between devices, swap(): return lax.ppermute(value, axis, [(i, i ^ mask) for i in range(count)])  47.3 us
    pallas_call x1, Pallas kernels, mid_bwd(): pl.pallas_call(functools.partial(mid_bwd_kernel, chunk=256, count=count,...  31.2 us
    pallas_call x1, Pallas kernels, attn_fwd(): pl.pallas_call(functools.partial(attn_fwd_kernel, block=512, count=count,...  27 us
    pallas_call x1, Pallas kernels, second_norm(): pl.pallas_call(functools.partial(second_norm_kernel, cores=len(downs), ti...  21.6 us
    pallas_call x1, Pallas kernels, mid_fwd(): pl.pallas_call(functools.partial(mid_fwd_kernel, chunk=256, count=count,...  20.9 us
    pallas_call x1, Pallas kernels, input_grad(): pl.pallas_call(functools.partial(input_grad_kernel, count=count, chunks=c...  10.8 us
  transfers between devices with their start and end apart: 50, of which 25 were waited for; matrix products, arithmetic and copies ran while one was open for 2% of the time, Pallas kernels for 51%

profile of v1, /device:TPU:0, one launch (start us, length us, event | category | flops | bytes accessed | tf_op | source)
XLA Modules:
  0.0 325.8 jit_solution(18170459354171375283)
XLA Ops:
  8.7 0.9 fusion.1.refs_0_
  9.6 5.1 %collective-permute-start.2 = (bf16[112,768]{1,0:T(8,128)(2,1)S(1)}, bf16[112,768]{1,0:T(8,128)(2,1)S(1)}, u32[]{:S(2)}, u32[]{:S(2)}) collective-permute-start(bf16[112,768]{1,0:T(8,128)(2,1)S(1)} %fusion.1.refs_0_), channel_id=1, source_target_pairs={{0,3},{1,2},{2,1},{3,0},{4,7},{5,6},{6,5},{7,4},{8,11},{9,10},{10,... | collective-permute-start | bytes 516104 | tf_op jit(solution)/shard_map/ppermute | solution.py:790
  15.9 3.1 turn.2.refs_4_.x_hbm
  19.0 1.0 collective-permute-done.2.refs_3_
  20.0 9.3 %collective-permute-done.1.refs_2_ = bf16[112,768]{1,0:T(8,128)(2,1)S(1)} collective-permute-done((bf16[112,768]{1,0:T(8,128)(2,1)S(1)}, bf16[112,768]{1,0:T(8,128)(2,1)S(1)}, u32[]{:S(2)}, u32[]{:S(2)}) %collective-permute-start.1) | collective-permute-done | bytes 172064 | tf_op jit(solution)/shard_map/ppermute | solution.py:790
  30.6 2.1 attention_weight_order.1
  32.7 1.5 collective-permute-start.3
  34.2 1.5 collective-permute-start.5
  36.2 2.5 collective-permute-start.8
  38.7 5.2 %collective-permute-done.8.refs_3_ = bf16[96,768]{1,0:T(8,128)(2,1)S(1)} collective-permute-done((bf16[96,768]{1,0:T(8,128)(2,1)S(1)}, bf16[96,768]{1,0:T(8,128)(2,1)S(1)}, u32[]{:S(2)}, u32[]{:S(2)}) %collective-permute-start.8) | collective-permute-done | bytes 147488 | tf_op jit(solution)/shard_map/ppermute | solution.py:790
  43.9 4.9 %collective-permute-start.6 = (bf16[96,768]{1,0:T(8,128)(2,1)S(1)}, bf16[96,768]{1,0:T(8,128)(2,1)S(1)}, u32[]{:S(2)}, u32[]{:S(2)}) collective-permute-start(bf16[96,768]{1,0:T(8,128)(2,1)S(1)} %copy-done.15), channel_id=1, source_target_pairs={{0,1},{1,0},{2,3},{3,2},{4,5},{5,4},{6,7},{7,6},{8,9},{9,8},{10,11... | collective-permute-start | bytes 442376 | tf_op jit(solution)/shard_map/ppermute | solution.py:790
  48.8 1.2 collective-permute-done.7.refs_2_
  50.0 2.0 collective-permute-done.6.refs_1_
  52.7 2.2 weight_order.1.refs_8_.refs_0_.refs_2_
  54.9 2.0 dynamic-slice_bitcast_fusion
  59.8 1.8 collective-permute-start.15
  61.6 1.1 collective-permute-start.14
  63.5 27.0 %attention_forward.1 = (bf16[1024,768]{1,0:T(8,128)(2,1)}, bf16[1024,768]{1,0:T(8,128)(2,1)}, bf16[1024,768]{1,0:T(8,128)(2,1)}, bf16[1024,768]{1,0:T(8,128)(2,1...) custom-call(s32[3]{0:T(128)} %pad_add_fusion.place_ref, s32[1]{0:T(128)S(6)} %copy.43.len_ref, f32[6]{0:T(128)} %scale_ref.9, ...), custom_call_target="tpu_custom_call" | custom-call | flops 20000000000 | bytes 12000000 | tf_op jit(solution)/shard_map/attention_forward/pallas_call | solution.py:264
  90.6 3.1 turn.3.refs_8_.c_hbm
  93.7 1.4 collective-permute-done.14.refs_2_.refs_4_
  95.7 2.5 collective-permute-done.17.refs_5_.refs_7_
  98.8 1.1 collective-permute-done.19.refs_7_.refs_9_
  99.8 20.9 %middle_forward.1 = (f32[1024,768]{1,0:T(8,128)}, f32[1024,128]{1,0:T(8,128)}, bf16[1024,768]{1,0:T(8,128)(2,1)}, bf16[1024,3072]{1,0:T(8,128)(2,1)}, bf16[1024,3072]{1,0:T(8,128)(2,1)}) custom-call(s32[3]{0:T(128)} %pad_add_fusion.place_ref, f32[6]{0:T(128)} %scale_ref.9, bf16[480,768]{1,0:T(8,128)(2,1)} %weight_order.1.refs_8_.refs_0_.refs_2_, ...), custom_call_target="tpu_custom_call" | custom-call | flops 12000000000 | bytes 25000000 | tf_op jit(solution)/shard_map/middle_forward/pallas_call | solution.py:521
  121.0 4.7 %collective-permute-done.20.refs_1_ = bf16[4,4,192,384]{3,2,1,0:T(8,128)(2,1)} collective-permute-done((bf16[4,4,192,384]{3,2,1,0:T(8,128)(2,1)}, bf16[4,4,192,384]{3,2,1,0:T(8,128)(2,1)}, u32[]{:S(2)}, u32[]{:S(2)}) %collective-permute-start.20) | collective-permute-done | bytes 2359328 | tf_op jit(solution)/shard_map/ppermute | solution.py:790
  125.7 21.6 %second_norm.1 = (bf16[1024,768]{1,0:T(8,128)(2,1)}, f32[1024,768]{1,0:T(8,128)}, bf16[1024,768]{1,0:T(8,128)(2,1)}, f32[8,768]{1,0:T(8,128)}, bf16[8,4,192,384]{3,2,1,0:T(8,128)(2,1)}) custom-call(s32[3]{0:T(128)} %pad_add_fusion.place_ref, f32[6]{0:T(128)} %scale_ref.9, bf16[4,4,192,384]{3,2,1,0:T(8,128)(2,1)} %bitcast.59, ...), custom_call_target="tpu_custom_call" | custom-call | flops 16000000000 | bytes 30000000 | tf_op jit(solution)/shard_map/second_norm/pallas_call | solution.py:616
  147.3 31.2 %middle_backward.1 = (f32[1024,768]{1,0:T(8,128)}, bf16[1024,768]{1,0:T(8,128)(2,1)}, bf16[1024,768]{1,0:T(8,128)(2,1)}, f32[8,768]{1,0:T(8,128)}, f32[8,3072]{1...) custom-call(s32[3]{0:T(128)} %pad_add_fusion.place_ref, f32[6]{0:T(128)} %scale_ref.9, ...), custom_call_target="tpu_custom_call" | custom-call | flops 28000000000 | bytes 40000000 | tf_op jit(solution)/shard_map/middle_backward/pallas_call | solution.py:718
  178.7 17.6 %attention_backward.3 = (bf16[4,4,96,256]{3,2,1,0:T(8,128)(2,1)}, bf16[4,4,96,256]{3,2,1,0:T(8,128)(2,1)}, bf16[1024,768]{1,0:T(8,128)(2,1)}, f32[16,256]{1,0:T(8,128)}) custom-call(s32[3]{0:T(128)} %pad_add_fusion.place_ref, s32[1]{0:T(128)S(6)} %copy.43.len_ref, bf16[1024,768]{1,0:T(8,128)(2,1)} %get-tuple-element.119.q_ref, ...), custom_call_target="tpu_custom_call" | custom-call | flops 16666667008 | bytes 10000000 | tf_op jit(solution)/shard_map/attention_backward/pallas_call | solution.py:452
  196.4 3.6 %core_sum.2 = (bf16[4,96,768]{2,1,0:T(8,128)(2,1)}, bf16[4,96,768]{2,1,0:T(8,128)(2,1)}, bf16[4,96,768]{2,1,0:T(8,128)(2,1)}, bf16[4,96,768]{2,1,0:T(8,128)(2,1)}) custom-call(bf16[4,4,96,768]{3,2,1,0:T(8,128)(2,1)} %get-tuple-element.131.refs_0_, bf16[4,4,96,768]{3,2,1,0:T(8,128)(2,1)} %collective-permute-done.21.refs_1_, ...), custom_call_target="tpu_custom_call" | custom-call | flops 1000000 | bytes 7077888 | tf_op jit(solution)/shard_map/core_sum/pallas_call | solution.py:848
  200.0 1.1 collective-permute-start.23
  201.1 2.3 collective-permute-start.24
  203.5 25.8 %attention_backward.4 = (bf16[4,4,96,384]{3,2,1,0:T(8,128)(2,1)}, bf16[4,4,96,384]{3,2,1,0:T(8,128)(2,1)}, bf16[1024,1152]{1,0:T(8,128)(2,1)}, f32[16,384]{1,0:T(8,128)}) custom-call(s32[3]{0:T(128)} %pad_add_fusion.place_ref, s32[1]{0:T(128)S(6)} %copy.43.len_ref, bf16[1024,768]{1,0:T(8,128)(2,1)} %get-tuple-element.119.q_ref, ...), custom_call_target="tpu_custom_call" | custom-call | flops 24999999488 | bytes 15000000 | tf_op jit(solution)/shard_map/attention_backward/pallas_call | solution.py:452
  229.5 0.7 copy-done.4
  230.6 2.7 plane_sum.2.refs_0_
  233.4 11.5 %attention_backward.5 = (bf16[4,4,112,128]{3,2,1,0:T(8,128)(2,1)}, bf16[4,4,112,128]{3,2,1,0:T(8,128)(2,1)}, bf16[1024,384]{1,0:T(8,128)(2,1)}, f32[16,768]{1,0:T(8,128)}) custom-call(s32[3]{0:T(128)} %pad_add_fusion.place_ref, s32[1]{0:T(128)S(6)} %copy.43.len_ref, bf16[1024,768]{1,0:T(8,128)(2,1)} %get-tuple-element.119.q_ref, ...), custom_call_target="tpu_custom_call" | custom-call | flops 8333333504 | bytes 5000000 | tf_op jit(solution)/shard_map/attention_backward/pallas_call | solution.py:452
  245.0 1.0 copy-done
  246.0 2.6 pair_sum.1.refs_4_
  248.6 3.7 %collective-permute-start.26 = (bf16[4,4,96,256]{3,2,1,0:T(8,128)(2,1)S(1)}, bf16[4,4,96,256]{3,2,1,0:T(8,128)(2,1)S(1)}, u32[]{:S(2)}, u32[]{:S(2)}) collective-permute-start(bf16[4,4,96,256]{3,2,1,0:T(8,128)(2,1)S(1)} %copy-done.25), channel_id=1, source_target_pairs={{0,4},{4,0},{8,12},{12,8},{16,20},{20,16},{24,28},{28,24},{1,5},{5... | collective-permute-start | bytes 2359304 | tf_op jit(solution)/shard_map/ppermute | solution.py:790
  252.4 2.2 collective-permute-done.26.refs_3_
  255.8 2.7 core_sum.3
  259.2 1.3 collective-permute-start.32
  260.5 1.6 collective-permute-start.33
  262.1 10.8 %input_gradient.1.refs_4_ = bf16[1024,768]{1,0:T(8,128)(2,1)} custom-call(s32[3]{0:T(128)} %pad_add_fusion.place_ref, f32[6]{0:T(128)} %scale_ref.9, bf16[304,768]{1,0:T(8,128)(2,1)} %get-tuple-element.106.refs_0_, bf16[304,768]{1,0:T(8,128)(2,1)} %copy-done.7, bf16[304,768]{1,0:T(8,128)(2,1)} %collective-permute-done.4.refs_2_, ...), custom_call_target="tpu_custom_call" | custom-call | flops 8999999488 | bytes 12976128 | tf_op jit(solution)/shard_map/input_gradient/pallas_call | solution.py:775
  272.9 3.7 %collective-permute-done.32.refs_2_ = bf16[4,112,384]{2,1,0:T(8,128)(2,1)S(1)} collective-permute-done((bf16[4,112,384]{2,1,0:T(8,128)(2,1)}, bf16[4,112,384]{2,1,0:T(8,128)(2,1)S(1)}, u32[]{:S(2)}, u32[]{:S(2)}) %collective-permute-start.32) | collective-permute-done | bytes 344096 | tf_op jit(solution)/shard_map/ppermute | solution.py:790
  276.6 0.7 copy-done.10
  277.4 0.7 copy-done.11
  278.1 2.1 plane_sum.3
  280.2 2.8 collective-permute-start.34
  283.1 2.4 collective-permute-start.36
  285.4 1.7 slice_bitcast_fusion
  287.1 2.7 collective-permute-start.31
  290.6 0.7 collective-permute-done.35.refs_6_
  291.3 1.1 collective-permute-done.31.refs_3_
  292.5 1.6 collective-permute-done.30.refs_2_
  295.1 2.2 own_sums.1
  297.3 1.4 collective-permute-done.37
  299.8 1.2 collective-permute-start.39
  301.1 1.7 collective-permute-start.38
  303.5 2.1 collective-permute-done.38
  305.6 1.1 collective-permute-start.43
  306.7 1.2 collective-permute-start.42
  307.9 2.1 collective-permute-start.41
  310.0 1.2 collective-permute-done.42
  311.2 2.0 collective-permute-done.41
  313.9 4.6 %state_update.1 = (f32[96,768]{1,0:T(8,128)}, f32[96,768]{1,0:T(8,128)}, f32[96,768]{1,0:T(8,128)}, f32[96,768]{1,0:T(8,128)}, f32[96,768]{1,0:T(8,128)}, /*inde...) custom-call(f32[8,128]{1,0:T(8,128)} %add_add_fusion.square_ref, ...), custom_call_target="tpu_custom_call" | custom-call | flops 10000000 | bytes 8000000 | tf_op jit(solution)/shard_map/state_update/pallas_call | solution.py:986
  (133 shorter events, 16.8 us)
Async XLA Ops:
  7.2 47.7 %all-gather.5.cloned.1.call-start = ((), (), s32[]{:S(2)}) async-start(), calls=%async_computation.8 | async-start | bytes 1327104 | tf_op jit(solution)/shard_map/all_gather | solution.py:1021
  7.9 112.8 %all-gather.7.cloned.1.call-start = ((), (), s32[]{:S(2)}) async-start(), calls=%async_computation.9 | async-start | bytes 2949120 | tf_op jit(solution)/shard_map/all_gather | solution.py:1024
  9.6 9.4 %copy-start.3 = (bf16[112,768]{1,0:T(8,128)(2,1)}, bf16[112,768]{1,0:T(8,128)(2,1)S(1)}, u32[]{:S(2)}) copy-start(bf16[112,768]{1,0:T(8,128)(2,1)S(1)} %fusion.1.refs_0_) | copy-start | bytes 516100
  9.6 10.4 %collective-permute-start.2 = (bf16[112,768]{1,0:T(8,128)(2,1)S(1)}, bf16[112,768]{1,0:T(8,128)(2,1)S(1)}, u32[]{:S(2)}, u32[]{:S(2)}) collective-permute-start(bf16[112,768]{1,0:T(8,128)(2,1)S(1)} %fusion.1.refs_0_), channel_id=1, source_target_pairs={{0,3},{1,2},{2,1},{3,0},{4,7},{5,6},{6,5},{7,4},{8,11},{9,10},{10,... | collective-permute-start | bytes 516104 | tf_op jit(solution)/shard_map/ppermute | solution.py:790
  14.7 14.6 %collective-permute-start.1 = (bf16[112,768]{1,0:T(8,128)(2,1)S(1)}, bf16[112,768]{1,0:T(8,128)(2,1)S(1)}, u32[]{:S(2)}, u32[]{:S(2)}) collective-permute-start(bf16[112,768]{1,0:T(8,128)(2,1)S(1)} %fusion.1.refs_0_), channel_id=1, source_target_pairs={{0,2},{1,3},{2,0},{3,1},{4,6},{5,7},{6,4},{7,5},{8,10},{9,11},{10,... | collective-permute-start | bytes 516104 | tf_op jit(solution)/shard_map/ppermute | solution.py:790
  14.7 14.6 %collective-permute-start = (bf16[112,768]{1,0:T(8,128)(2,1)S(1)}, bf16[112,768]{1,0:T(8,128)(2,1)S(1)}, u32[]{:S(2)}, u32[]{:S(2)}) collective-permute-start(bf16[112,768]{1,0:T(8,128)(2,1)S(1)} %fusion.1.refs_0_), channel_id=1, source_target_pairs={{0,1},{1,0},{2,3},{3,2},{4,5},{5,4},{6,7},{7,6},{8,9},{9,8},{10,11... | collective-permute-start | bytes 516104 | tf_op jit(solution)/shard_map/ppermute | solution.py:790
  19.0 17.2 %copy-start.15 = (bf16[96,768]{1,0:T(8,128)(2,1)S(1)}, bf16[96,768]{1,0:T(8,128)(2,1)}, u32[]{:S(2)}) copy-start(bf16[96,768]{1,0:T(8,128)(2,1)} %refs_0_.1) | copy-start | bytes 442372
  20.0 9.3 %copy-start.12 = (bf16[112,768]{1,0:T(8,128)(2,1)}, bf16[112,768]{1,0:T(8,128)(2,1)S(1)}, u32[]{:S(2)}) copy-start(bf16[112,768]{1,0:T(8,128)(2,1)S(1)} %collective-permute-done.2.refs_3_) | copy-start | bytes 516100
  32.7 24.6 %copy-start.28 = (bf16[304,768]{1,0:T(8,128)(2,1)S(1)}, bf16[304,768]{1,0:T(8,128)(2,1)}, u32[]{:S(2)}) copy-start(bf16[304,768]{1,0:T(8,128)(2,1)} %get-tuple-element.106.refs_0_) | copy-start | bytes 1400836
  32.7 19.2 %collective-permute-start.3 = (bf16[304,768]{1,0:T(8,128)(2,1)}, bf16[304,768]{1,0:T(8,128)(2,1)S(1)}, u32[]{:S(2)}, u32[]{:S(2)}) collective-permute-start(bf16[304,768]{1,0:T(8,128)(2,1)} %get-tuple-element.106.refs_0_), channel_id=1, source_target_pairs={{0,8},{4,12},{8,0},{12,4},{16,24},{20,28},{24,16},{28,20},{1,9},{5... | collective-permute-start | bytes 1400840 | tf_op jit(solution)/shard_map/ppermute | solution.py:790
  34.2 22.7 %collective-permute-start.5 = (bf16[304,768]{1,0:T(8,128)(2,1)}, bf16[304,768]{1,0:T(8,128)(2,1)}, u32[]{:S(2)}, u32[]{:S(2)}) collective-permute-start(bf16[304,768]{1,0:T(8,128)(2,1)} %get-tuple-element.106.refs_0_), channel_id=1, source_target_pairs={{0,24},{4,28},{8,16},{12,20},{16,8},{20,12},{24,0},{28,4},{1,25},{... | collective-permute-start | bytes 1400840 | tf_op jit(solution)/shard_map/ppermute | solution.py:790
  35.7 21.6 %collective-permute-start.4 = (bf16[304,768]{1,0:T(8,128)(2,1)}, bf16[304,768]{1,0:T(8,128)(2,1)}, u32[]{:S(2)}, u32[]{:S(2)}) collective-permute-start(bf16[304,768]{1,0:T(8,128)(2,1)} %get-tuple-element.106.refs_0_), channel_id=1, source_target_pairs={{0,16},{4,20},{8,24},{12,28},{16,0},{20,4},{24,8},{28,12},{1,17},{... | collective-permute-start | bytes 1400840 | tf_op jit(solution)/shard_map/ppermute | solution.py:790
  36.2 7.6 %collective-permute-start.8 = (bf16[96,768]{1,0:T(8,128)(2,1)S(1)}, bf16[96,768]{1,0:T(8,128)(2,1)S(1)}, u32[]{:S(2)}, u32[]{:S(2)}) collective-permute-start(bf16[96,768]{1,0:T(8,128)(2,1)S(1)} %copy-done.15), channel_id=1, source_target_pairs={{0,3},{1,2},{2,1},{3,0},{4,7},{5,6},{6,5},{7,4},{8,11},{9,10},{10,... | collective-permute-start | bytes 442376 | tf_op jit(solution)/shard_map/ppermute | solution.py:790
  38.7 11.2 %collective-permute-start.7 = (bf16[96,768]{1,0:T(8,128)(2,1)S(1)}, bf16[96,768]{1,0:T(8,128)(2,1)S(1)}, u32[]{:S(2)}, u32[]{:S(2)}) collective-permute-start(bf16[96,768]{1,0:T(8,128)(2,1)S(1)} %copy-done.15), channel_id=1, source_target_pairs={{0,2},{1,3},{2,0},{3,1},{4,6},{5,7},{6,4},{7,5},{8,10},{9,11},{10,... | collective-permute-start | bytes 442376 | tf_op jit(solution)/shard_map/ppermute | solution.py:790
  43.9 8.1 %copy-start.16 = (bf16[96,768]{1,0:T(8,128)(2,1)}, bf16[96,768]{1,0:T(8,128)(2,1)S(1)}, u32[]{:S(2)}) copy-start(bf16[96,768]{1,0:T(8,128)(2,1)S(1)} %collective-permute-done.8.refs_3_) | copy-start | bytes 442372
  43.9 8.0 %collective-permute-start.6 = (bf16[96,768]{1,0:T(8,128)(2,1)S(1)}, bf16[96,768]{1,0:T(8,128)(2,1)S(1)}, u32[]{:S(2)}, u32[]{:S(2)}) collective-permute-start(bf16[96,768]{1,0:T(8,128)(2,1)S(1)} %copy-done.15), channel_id=1, source_target_pairs={{0,1},{1,0},{2,3},{3,2},{4,5},{5,4},{6,7},{7,6},{8,9},{9,8},{10,11... | collective-permute-start | bytes 442376 | tf_op jit(solution)/shard_map/ppermute | solution.py:790
  54.9 4.9 %copy-start.2 = (bf16[480,768]{1,0:T(8,128)(2,1)S(1)}, bf16[480,768]{1,0:T(8,128)(2,1)}, u32[]{:S(2)}) copy-start(bf16[480,768]{1,0:T(8,128)(2,1)} %weight_order.1.refs_8_.refs_0_.refs_2_) | copy-start | bytes 2211844
  57.3 2.5 collective-permute-start.10
  57.3 4.3 %collective-permute-start.11 = (bf16[304,768]{1,0:T(8,128)(2,1)}, bf16[304,768]{1,0:T(8,128)(2,1)S(1)}, u32[]{:S(2)}, u32[]{:S(2)}) collective-permute-start(bf16[304,768]{1,0:T(8,128)(2,1)} %copy-done.7), channel_id=1, source_target_pairs={{0,4},{4,0},{8,12},{12,8},{16,20},{20,16},{24,28},{28,24},{1,5},{5... | collective-permute-start | bytes 1400840 | tf_op jit(solution)/shard_map/ppermute | solution.py:790
  57.8 4.9 %collective-permute-start.12 = (bf16[304,768]{1,0:T(8,128)(2,1)}, bf16[304,768]{1,0:T(8,128)(2,1)S(1)}, u32[]{:S(2)}, u32[]{:S(2)}) collective-permute-start(bf16[304,768]{1,0:T(8,128)(2,1)} %collective-permute-done.4.refs_2_), channel_id=1, source_target_pairs={{0,4},{4,0},{8,12},{12,8},{16,20},{20,16},{24,28},{28,24},{1,5},{5... | collective-permute-start | bytes 1400840 | tf_op jit(solution)/shard_map/ppermute | solution.py:790
  57.8 5.7 %collective-permute-start.13 = (bf16[304,768]{1,0:T(8,128)(2,1)}, bf16[304,768]{1,0:T(8,128)(2,1)}, u32[]{:S(2)}, u32[]{:S(2)}) collective-permute-start(bf16[304,768]{1,0:T(8,128)(2,1)} %collective-permute-done.5.refs_3_), channel_id=1, source_target_pairs={{0,4},{4,0},{8,12},{12,8},{16,20},{20,16},{24,28},{28,24},{1,5},{5... | collective-permute-start | bytes 1400840 | tf_op jit(solution)/shard_map/ppermute | solution.py:790
  59.0 36.7 %collective-permute-start.16 = (bf16[480,768]{1,0:T(8,128)(2,1)}, bf16[480,768]{1,0:T(8,128)(2,1)S(1)}, u32[]{:S(2)}, u32[]{:S(2)}) collective-permute-start(bf16[480,768]{1,0:T(8,128)(2,1)} %weight_order.1.refs_8_.refs_0_.refs_2_), channel_id=1, source_target_pairs={{0,4},{4,0},{8,12},{12,8},{16,20},{20,16},{24,28},{28,24},{1,5},{5... | collective-permute-start | bytes 2211848 | tf_op jit(solution)/shard_map/ppermute | solution.py:790
  59.1 144.4 %reduce-scatter.5.cloned.1.call-start = ((), (), s32[]{:S(2)}) async-start(), calls=%async_computation.4 | async-start | bytes 5308416 | tf_op jit(solution)/shard_map/reduce_scatter | solution.py:1061
  59.8 3.6 %copy-start.29 = (bf16[304,768]{1,0:T(8,128)(2,1)}, bf16[304,768]{1,0:T(8,128)(2,1)S(1)}, u32[]{:S(2)}) copy-start(bf16[304,768]{1,0:T(8,128)(2,1)S(1)} %collective-permute-done.10.refs_4_) | copy-start | bytes 1400836
  59.8 33.9 %collective-permute-start.15 = (bf16[480,768]{1,0:T(8,128)(2,1)S(1)}, bf16[480,768]{1,0:T(8,128)(2,1)}, u32[]{:S(2)}, u32[]{:S(2)}) collective-permute-start(bf16[480,768]{1,0:T(8,128)(2,1)S(1)} %copy-done.2), channel_id=1, source_target_pairs={{0,24},{4,28},{8,16},{12,20},{16,8},{20,12},{24,0},{28,4},{1,25},{... | collective-permute-start | bytes 2211848 | tf_op jit(solution)/shard_map/ppermute | solution.py:790
  61.6 33.5 %collective-permute-start.14 = (bf16[480,768]{1,0:T(8,128)(2,1)S(1)}, bf16[480,768]{1,0:T(8,128)(2,1)}, u32[]{:S(2)}, u32[]{:S(2)}) collective-permute-start(bf16[480,768]{1,0:T(8,128)(2,1)S(1)} %copy-done.2), channel_id=1, source_target_pairs={{0,16},{4,20},{8,24},{12,28},{16,0},{20,4},{24,8},{28,12},{1,17},{... | collective-permute-start | bytes 2211848 | tf_op jit(solution)/shard_map/ppermute | solution.py:790
  62.7 32.4 %collective-permute-start.9 = (bf16[480,768]{1,0:T(8,128)(2,1)S(1)}, bf16[480,768]{1,0:T(8,128)(2,1)}, u32[]{:S(2)}, u32[]{:S(2)}) collective-permute-start(bf16[480,768]{1,0:T(8,128)(2,1)S(1)} %copy-done.2), channel_id=1, source_target_pairs={{0,8},{4,12},{8,0},{12,4},{16,24},{20,28},{24,16},{28,20},{1,9},{5... | collective-permute-start | bytes 2211848 | tf_op jit(solution)/shard_map/ppermute | solution.py:790
  95.1 3.1 collective-permute-start.17
  95.2 3.6 %collective-permute-start.18 = (bf16[480,768]{1,0:T(8,128)(2,1)}, bf16[480,768]{1,0:T(8,128)(2,1)}, u32[]{:S(2)}, u32[]{:S(2)}) collective-permute-start(bf16[480,768]{1,0:T(8,128)(2,1)} %collective-permute-done.14.refs_2_.refs_4_), channel_id=1, source_target_pairs={{0,4},{4,0},{8,12},{12,8},{16,20},{20,16},{24,28},{28,24},{1,5},{5... | collective-permute-start | bytes 2211848 | tf_op jit(solution)/shard_map/ppermute | solution.py:790
  95.6 4.2 %collective-permute-start.19 = (bf16[480,768]{1,0:T(8,128)(2,1)}, bf16[480,768]{1,0:T(8,128)(2,1)}, u32[]{:S(2)}, u32[]{:S(2)}) collective-permute-start(bf16[480,768]{1,0:T(8,128)(2,1)} %collective-permute-done.15.refs_3_.refs_5_), channel_id=1, source_target_pairs={{0,4},{4,0},{8,12},{12,8},{16,20},{20,16},{24,28},{28,24},{1,5},{5... | collective-permute-start | bytes 2211848 | tf_op jit(solution)/shard_map/ppermute | solution.py:790
  95.7 4.1 %copy-start.26 = (bf16[480,768]{1,0:T(8,128)(2,1)}, bf16[480,768]{1,0:T(8,128)(2,1)S(1)}, u32[]{:S(2)}) copy-start(bf16[480,768]{1,0:T(8,128)(2,1)S(1)} %collective-permute-done.16.refs_4_.refs_6_) | copy-start | bytes 2211844
  120.7 4.9 %collective-permute-start.20 = (bf16[4,4,192,384]{3,2,1,0:T(8,128)(2,1)}, bf16[4,4,192,384]{3,2,1,0:T(8,128)(2,1)}, u32[]{:S(2)}, u32[]{:S(2)}) collective-permute-start(bf16[4,4,192,384]{3,2,1,0:T(8,128)(2,1)} %bitcast.58), channel_id=1, source_target_pairs={{0,4},{4,0},{8,12},{12,8},{16,20},{20,16},{24,28},{28,24},{1,5},{5... | collective-permute-start | bytes 7077896 | tf_op jit(solution)/shard_map/ppermute | solution.py:790
  147.3 82.2 %reduce-scatter.7.cloned.1.call-start = ((), (), s32[]{:S(2)}) async-start(), calls=%async_computation.5 | async-start | bytes 737280 | tf_op jit(solution)/shard_map/reduce_scatter | solution.py:1068
  178.5 17.8 %collective-permute-start.21 = (bf16[4,4,96,768]{3,2,1,0:T(8,128)(2,1)}, bf16[4,4,96,768]{3,2,1,0:T(8,128)(2,1)}, u32[]{:S(2)}, u32[]{:S(2)}) collective-permute-start(bf16[4,4,96,768]{3,2,1,0:T(8,128)(2,1)} %get-tuple-element.132.refs_0_), channel_id=1, source_target_pairs={{0,4},{4,0},{8,12},{12,8},{16,20},{20,16},{24,28},{28,24},{1,5},{5... | collective-permute-start | bytes 7077896 | tf_op jit(solution)/shard_map/ppermute | solution.py:790
  200.0 29.4 %collective-permute-start.22 = (bf16[4,96,768]{2,1,0:T(8,128)(2,1)}, bf16[4,96,768]{2,1,0:T(8,128)(2,1)S(1)}, u32[]{:S(2)}, u32[]{:S(2)}) collective-permute-start(bf16[4,96,768]{2,1,0:T(8,128)(2,1)} %get-tuple-element.136), channel_id=1, source_target_pairs={{0,8},{4,12},{8,0},{12,4},{16,24},{20,28},{24,16},{28,20},{1,9},{5... | collective-permute-start | bytes 1769480 | tf_op jit(solution)/shard_map/ppermute | solution.py:790
  200.0 29.4 %collective-permute-start.23 = (bf16[4,96,768]{2,1,0:T(8,128)(2,1)}, bf16[4,96,768]{2,1,0:T(8,128)(2,1)S(1)}, u32[]{:S(2)}, u32[]{:S(2)}) collective-permute-start(bf16[4,96,768]{2,1,0:T(8,128)(2,1)} %get-tuple-element.137), channel_id=1, source_target_pairs={{0,16},{4,20},{8,24},{12,28},{16,0},{20,4},{24,8},{28,12},{1,17},{... | collective-permute-start | bytes 1769480 | tf_op jit(solution)/shard_map/ppermute | solution.py:790
  201.1 28.3 %collective-permute-start.24 = (bf16[4,96,768]{2,1,0:T(8,128)(2,1)}, bf16[4,96,768]{2,1,0:T(8,128)(2,1)S(1)}, u32[]{:S(2)}, u32[]{:S(2)}) collective-permute-start(bf16[4,96,768]{2,1,0:T(8,128)(2,1)} %get-tuple-element.138), channel_id=1, source_target_pairs={{0,24},{4,28},{8,16},{12,20},{16,8},{20,12},{24,0},{28,4},{1,25},{... | collective-permute-start | bytes 1769480 | tf_op jit(solution)/shard_map/ppermute | solution.py:790
  203.5 51.6 %reduce-scatter.9.cloned.1.call-start = ((), (), s32[]{:S(2)}) async-start(), calls=%async_computation.6 | async-start | bytes 737280 | tf_op jit(solution)/shard_map/reduce_scatter | solution.py:1070
  233.3 11.6 %collective-permute-start.27 = (bf16[4,4,96,384]{3,2,1,0:T(8,128)(2,1)}, bf16[4,4,96,384]{3,2,1,0:T(8,128)(2,1)S(1)}, u32[]{:S(2)}, u32[]{:S(2)}) collective-permute-start(bf16[4,4,96,384]{3,2,1,0:T(8,128)(2,1)} %get-tuple-element.152), channel_id=1, source_target_pairs={{0,4},{4,0},{8,12},{12,8},{16,20},{20,16},{24,28},{28,24},{1,5},{5... | collective-permute-start | bytes 3538952 | tf_op jit(solution)/shard_map/ppermute | solution.py:790
  233.4 52.1 %reduce-scatter.11.cloned.1.call-start = ((), (), s32[]{:S(2)}) async-start(), calls=%async_computation.7 | async-start | bytes 1474560 | tf_op jit(solution)/shard_map/reduce_scatter | solution.py:1077
  246.0 2.6 copy-start.25
  248.6 5.9 %collective-permute-start.26 = (bf16[4,4,96,256]{3,2,1,0:T(8,128)(2,1)S(1)}, bf16[4,4,96,256]{3,2,1,0:T(8,128)(2,1)S(1)}, u32[]{:S(2)}, u32[]{:S(2)}) collective-permute-start(bf16[4,4,96,256]{3,2,1,0:T(8,128)(2,1)S(1)} %copy-done.25), channel_id=1, source_target_pairs={{0,4},{4,0},{8,12},{12,8},{16,20},{20,16},{24,28},{28,24},{1,5},{5... | collective-permute-start | bytes 2359304 | tf_op jit(solution)/shard_map/ppermute | solution.py:790
  252.3 2.8 collective-permute-start.25
  258.6 14.4 %collective-permute-start.28 = (bf16[4,112,384]{2,1,0:T(8,128)(2,1)}, bf16[4,112,384]{2,1,0:T(8,128)(2,1)S(1)}, u32[]{:S(2)}, u32[]{:S(2)}) collective-permute-start(bf16[4,112,384]{2,1,0:T(8,128)(2,1)} %get-tuple-element.155), channel_id=1, source_target_pairs={{0,8},{4,12},{8,0},{12,4},{16,24},{20,28},{24,16},{28,20},{1,9},{5... | collective-permute-start | bytes 1032200 | tf_op jit(solution)/shard_map/ppermute | solution.py:790
  259.2 17.4 %collective-permute-start.32 = (bf16[4,112,384]{2,1,0:T(8,128)(2,1)}, bf16[4,112,384]{2,1,0:T(8,128)(2,1)S(1)}, u32[]{:S(2)}, u32[]{:S(2)}) collective-permute-start(bf16[4,112,384]{2,1,0:T(8,128)(2,1)} %get-tuple-element.157), channel_id=1, source_target_pairs={{0,16},{4,20},{8,24},{12,28},{16,0},{20,4},{24,8},{28,12},{1,17},{... | collective-permute-start | bytes 1032200 | tf_op jit(solution)/shard_map/ppermute | solution.py:790
  260.5 16.1 %collective-permute-start.33 = (bf16[4,112,384]{2,1,0:T(8,128)(2,1)}, bf16[4,112,384]{2,1,0:T(8,128)(2,1)S(1)}, u32[]{:S(2)}, u32[]{:S(2)}) collective-permute-start(bf16[4,112,384]{2,1,0:T(8,128)(2,1)} %get-tuple-element.158), channel_id=1, source_target_pairs={{0,24},{4,28},{8,16},{12,20},{16,8},{20,12},{24,0},{28,4},{1,25},{... | collective-permute-start | bytes 1032200 | tf_op jit(solution)/shard_map/ppermute | solution.py:790
  272.9 3.7 %copy-start.9 = (bf16[4,112,384]{2,1,0:T(8,128)(2,1)}, bf16[4,112,384]{2,1,0:T(8,128)(2,1)S(1)}, u32[]{:S(2)}) copy-start(bf16[4,112,384]{2,1,0:T(8,128)(2,1)S(1)} %collective-permute-done.28.refs_1_) | copy-start | bytes 1032196
  280.2 9.9 %collective-permute-start.34 = (bf16[112,384]{1,0:T(8,128)(2,1)}, bf16[112,384]{1,0:T(8,128)(2,1)S(1)}, u32[]{:S(2)}, u32[]{:S(2)}) collective-permute-start(bf16[112,384]{1,0:T(8,128)(2,1)} %get-tuple-element.160), channel_id=1, source_target_pairs={{0,1},{1,0},{2,3},{3,2},{4,5},{5,4},{6,7},{7,6},{8,9},{9,8},{10,11... | collective-permute-start | bytes 258056 | tf_op jit(solution)/shard_map/ppermute | solution.py:790
  283.0 8.3 %collective-permute-start.35 = (bf16[112,384]{1,0:T(8,128)(2,1)}, bf16[112,384]{1,0:T(8,128)(2,1)S(1)}, u32[]{:S(2)}, u32[]{:S(2)}) collective-permute-start(bf16[112,384]{1,0:T(8,128)(2,1)} %get-tuple-element.161), channel_id=1, source_target_pairs={{0,2},{1,3},{2,0},{3,1},{4,6},{5,7},{6,4},{7,5},{8,10},{9,11},{10,... | collective-permute-start | bytes 258056 | tf_op jit(solution)/shard_map/ppermute | solution.py:790
  283.1 8.3 %collective-permute-start.36 = (bf16[112,384]{1,0:T(8,128)(2,1)}, bf16[112,384]{1,0:T(8,128)(2,1)S(1)}, u32[]{:S(2)}, u32[]{:S(2)}) collective-permute-start(bf16[112,384]{1,0:T(8,128)(2,1)} %get-tuple-element.162), channel_id=1, source_target_pairs={{0,3},{1,2},{2,1},{3,0},{4,7},{5,6},{6,5},{7,4},{8,11},{9,10},{10,... | collective-permute-start | bytes 258056 | tf_op jit(solution)/shard_map/ppermute | solution.py:790
  287.1 5.4 %collective-permute-start.31 = (bf16[96,384]{1,0:T(8,128)(2,1)S(1)}, bf16[96,384]{1,0:T(8,128)(2,1)S(1)}, u32[]{:S(2)}, u32[]{:S(2)}) collective-permute-start(bf16[96,384]{1,0:T(8,128)(2,1)S(1)} %get-tuple-element.183), channel_id=1, source_target_pairs={{0,24},{4,28},{8,16},{12,20},{16,8},{20,12},{24,0},{28,4},{1,25},{... | collective-permute-start | bytes 221192 | tf_op jit(solution)/shard_map/ppermute | solution.py:790
  289.7 4.4 %collective-permute-start.30 = (bf16[96,384]{1,0:T(8,128)(2,1)S(1)}, bf16[96,384]{1,0:T(8,128)(2,1)S(1)}, u32[]{:S(2)}, u32[]{:S(2)}) collective-permute-start(bf16[96,384]{1,0:T(8,128)(2,1)S(1)} %get-tuple-element.184), channel_id=1, source_target_pairs={{0,16},{4,20},{8,24},{12,28},{16,0},{20,4},{24,8},{28,12},{1,17},{... | collective-permute-start | bytes 221192 | tf_op jit(solution)/shard_map/ppermute | solution.py:790
  290.1 4.4 %copy-start.19 = (bf16[112,384]{1,0:T(8,128)(2,1)}, bf16[112,384]{1,0:T(8,128)(2,1)S(1)}, u32[]{:S(2)}) copy-start(bf16[112,384]{1,0:T(8,128)(2,1)S(1)} %collective-permute-done.34.refs_5_) | copy-start | bytes 258052
  290.1 4.4 %collective-permute-start.29 = (bf16[96,384]{1,0:T(8,128)(2,1)S(1)}, bf16[96,384]{1,0:T(8,128)(2,1)S(1)}, u32[]{:S(2)}, u32[]{:S(2)}) collective-permute-start(bf16[96,384]{1,0:T(8,128)(2,1)S(1)} %get-tuple-element.185), channel_id=1, source_target_pairs={{0,8},{4,12},{8,0},{12,4},{16,24},{20,28},{24,16},{28,20},{1,9},{5... | collective-permute-start | bytes 221192 | tf_op jit(solution)/shard_map/ppermute | solution.py:790
  291.3 3.1 copy-start.20
  291.3 3.1 copy-start.21
  292.4 2.0 copy-start.22
  297.3 1.4 collective-permute-start.37
  299.3 3.6 %collective-permute-start.40 = (f32[8,128]{1,0:T(8,128)S(1)}, f32[8,128]{1,0:T(8,128)S(1)}, u32[]{:S(2)}, u32[]{:S(2)}) collective-permute-start(f32[8,128]{1,0:T(8,128)S(1)} %add.36), channel_id=1, source_target_pairs={{0,8},{4,12},{8,0},{12,4},{16,24},{20,28},{24,16},{28,20},{1,9},{5... | collective-permute-start | bytes 12296 | tf_op jit(solution)/shard_map/ppermute | solution.py:790
  299.8 3.6 %collective-permute-start.39 = (f32[8,128]{1,0:T(8,128)S(1)}, f32[8,128]{1,0:T(8,128)S(1)}, u32[]{:S(2)}, u32[]{:S(2)}) collective-permute-start(f32[8,128]{1,0:T(8,128)S(1)} %add.36), channel_id=1, source_target_pairs={{0,16},{4,20},{8,24},{12,28},{16,0},{20,4},{24,8},{28,12},{1,17},{... | collective-permute-start | bytes 12296 | tf_op jit(solution)/shard_map/ppermute | solution.py:790
  301.1 4.5 %collective-permute-start.38 = (f32[8,128]{1,0:T(8,128)S(1)}, f32[8,128]{1,0:T(8,128)S(1)}, u32[]{:S(2)}, u32[]{:S(2)}) collective-permute-start(f32[8,128]{1,0:T(8,128)S(1)} %add.36), channel_id=1, source_target_pairs={{0,24},{4,28},{8,16},{12,20},{16,8},{20,12},{24,0},{28,4},{1,25},{... | collective-permute-start | bytes 12296 | tf_op jit(solution)/shard_map/ppermute | solution.py:790
  305.6 4.4 %collective-permute-start.43 = (f32[8,128]{1,0:T(8,128)S(1)}, f32[8,128]{1,0:T(8,128)S(1)}, u32[]{:S(2)}, u32[]{:S(2)}) collective-permute-start(f32[8,128]{1,0:T(8,128)S(1)} %add_add_fusion.1), channel_id=1, source_target_pairs={{0,1},{1,0},{2,3},{3,2},{4,5},{5,4},{6,7},{7,6},{8,9},{9,8},{10,11... | collective-permute-start | bytes 12296 | tf_op jit(solution)/shard_map/ppermute | solution.py:790
  306.7 4.5 %collective-permute-start.42 = (f32[8,128]{1,0:T(8,128)S(1)}, f32[8,128]{1,0:T(8,128)S(1)}, u32[]{:S(2)}, u32[]{:S(2)}) collective-permute-start(f32[8,128]{1,0:T(8,128)S(1)} %add_add_fusion.1), channel_id=1, source_target_pairs={{0,2},{1,3},{2,0},{3,1},{4,6},{5,7},{6,4},{7,5},{8,10},{9,11},{10,... | collective-permute-start | bytes 12296 | tf_op jit(solution)/shard_map/ppermute | solution.py:790
  307.9 5.4 %collective-permute-start.41 = (f32[8,128]{1,0:T(8,128)S(1)}, f32[8,128]{1,0:T(8,128)S(1)}, u32[]{:S(2)}, u32[]{:S(2)}) collective-permute-start(f32[8,128]{1,0:T(8,128)S(1)} %add_add_fusion.1), channel_id=1, source_target_pairs={{0,3},{1,2},{2,1},{3,0},{4,7},{5,6},{6,5},{7,4},{8,11},{9,10},{10,... | collective-permute-start | bytes 12296 | tf_op jit(solution)/shard_map/ppermute | solution.py:790
  (18 other events, 17.3 us)
Sparse Core Ops, SparseCore 0:
  9.9 27.0 all-gather.4
  59.2 49.9 all-gather.6
  147.4 53.1 reduce-scatter.4
  203.6 21.2 reduce-scatter.6
  233.5 21.3 reduce-scatter.8
  257.1 28.1 reduce-scatter.10
